TPU v7x, 256 devices: a whole 4x4x8 slice. The times are simulated.
256 devices in a mesh: tm: 8 (over z), seq: 32 (over x, y, core).
Axes of the slice: x: 4, y: 4, z: 8, core: 2. Of those that a mesh axis runs over, the one named last changes fastest.
Arguments:
- query_in: bfloat16 [32768, 512], P(('tm', 'seq')), may hold values from -30 to 30
- key_in: bfloat16 [32768, 128], P(('tm', 'seq')), may hold values from -6 to 6
- value_in: bfloat16 [32768, 128], P(('tm', 'seq')), may hold values from -6 to 6
- clean_keys: bfloat16 [32768, 128], P(('tm', 'seq')), may hold values from -6 to 6
- clean_values: bfloat16 [32768, 128], P(('tm', 'seq')), may hold values from -6 to 6
- timestep: int32 [8], P('tm'), may hold values from 0 to 999
- mod_table: float32 [1000, 512], replicated, may hold values from 0.5 to 3
- out_grad: bfloat16 [32768, 512], P(('tm', 'seq')), may hold values from -6 to 6
Outputs:
- gated_out: float32 [32768, 512], P(('tm', 'seq'))
- query_grad: float32 [32768, 512], P(('tm', 'seq'))
- key_grad: float32 [32768, 128], P(('tm', 'seq'))
- value_grad: float32 [32768, 128], P(('tm', 'seq'))
All inputs are finite; a program needn't handle non-finite values.
Results may differ from a plain program's by a relative error of at most 0.04.
Values may be sent and summed in bfloat16 or wider, within the bound.
A program may use at most 128 MiB of HBM per device.

v0:
```python
import math

import jax
import jax.numpy as jnp
from jax import lax
from jax.sharding import PartitionSpec as P


def contract_rows(left, right):
    return lax.dot_general(
        left, right, (((1,), (1,)), ((), ())), preferred_element_type=jnp.float32
    )


def contract_cols(left, right):
    return lax.dot_general(
        left, right, (((0,), (0,)), ((), ())), preferred_element_type=jnp.float32
    )


def attend_block(carried, queries, key_rows, value_rows, score_scale):
    peak, total, accum = carried
    scores = contract_rows(queries, key_rows) * score_scale
    fresh = jnp.maximum(peak, jnp.max(scores, axis=1))
    decay = jnp.exp(peak - fresh)
    expo = jnp.exp(scores - fresh[:, None])
    total = decay * total + jnp.sum(expo, axis=1)
    accum = decay[:, None] * accum + jnp.dot(
        expo.astype(jnp.bfloat16), value_rows, preferred_element_type=jnp.float32
    )
    return (fresh, total, accum)


def backward_block(queries, grad_rows, lse, delta, key_rows, value_rows, score_scale):
    scores = contract_rows(queries, key_rows) * score_scale
    probs = jnp.exp(scores - lse[:, None])
    dprob = contract_rows(grad_rows, value_rows)
    dscore = (probs * (dprob - delta[:, None]) * score_scale).astype(jnp.bfloat16)
    return (probs.astype(jnp.bfloat16), dscore)


def body(query_in, key_in, value_in, clean_keys, clean_values, timestep, mod_table, out_grad):
    local_rows, width = query_in.shape
    head_dim = key_in.shape[1]
    head_count = width // head_dim
    score_scale = 1.0 / math.sqrt(head_dim)
    group_index = lax.axis_index("tm")
    own_keys, own_values = (
        lax.all_gather(key_in, "seq", axis=0, tiled=True),
        lax.all_gather(value_in, "seq", axis=0, tiled=True),
    )
    past_keys, past_values = (
        lax.all_gather(clean_keys, ("tm", "seq"), axis=0, tiled=True),
        lax.all_gather(clean_values, ("tm", "seq"), axis=0, tiled=True),
    )
    group_span = own_keys.shape[0]
    key_block = math.gcd(group_span, 1024)
    own_steps = group_span // key_block
    past_steps = group_index * own_steps
    picker = (lax.iota(jnp.int32, mod_table.shape[0]) == timestep[0]).astype(jnp.float32)[None, :]
    gain = jnp.dot(
        picker, mod_table, precision=lax.Precision.HIGHEST, preferred_element_type=jnp.float32
    )
    query_rows = query_in.reshape(local_rows * head_count, head_dim)
    row_count = query_rows.shape[0]

    def past_forward(stride, carried):
        start = stride * key_block
        key_rows = lax.dynamic_slice_in_dim(past_keys, start, key_block, 0)
        value_rows = lax.dynamic_slice_in_dim(past_values, start, key_block, 0)
        return attend_block(carried, query_rows, key_rows, value_rows, score_scale)

    def own_forward(stride, carried):
        start = stride * key_block
        key_rows = lax.dynamic_slice_in_dim(own_keys, start, key_block, 0)
        value_rows = lax.dynamic_slice_in_dim(own_values, start, key_block, 0)
        return attend_block(carried, query_rows, key_rows, value_rows, score_scale)

    initial = (
        jnp.full((row_count,), -jnp.inf, jnp.float32),
        jnp.zeros((row_count,), jnp.float32),
        jnp.zeros((row_count, head_dim), jnp.float32),
    )
    carried = lax.fori_loop(0, past_steps, past_forward, initial)
    peak, total, accum = lax.fori_loop(0, own_steps, own_forward, carried)
    attended = (accum / total[:, None]).astype(jnp.bfloat16)
    gated_out = gain * attended.reshape(local_rows, width).astype(jnp.float32)
    grads = (gain * out_grad.astype(jnp.float32)).astype(jnp.bfloat16)
    grad_rows = grads.reshape(row_count, head_dim)
    delta = jnp.sum(grad_rows.astype(jnp.float32) * attended.astype(jnp.float32), axis=1)
    lse = peak + jnp.log(total)

    def past_backward(stride, qgrad):
        start = stride * key_block
        key_rows = lax.dynamic_slice_in_dim(past_keys, start, key_block, 0)
        value_rows = lax.dynamic_slice_in_dim(past_values, start, key_block, 0)
        prob_half, dscore = backward_block(
            query_rows, grad_rows, lse, delta, key_rows, value_rows, score_scale
        )
        return qgrad + jnp.dot(dscore, key_rows, preferred_element_type=jnp.float32)

    qgrad = lax.fori_loop(
        0, past_steps, past_backward, jnp.zeros((row_count, head_dim), jnp.float32)
    )

    def own_backward(stride, pair):
        qgrad_now, partial_grads = pair
        start = stride * key_block
        key_rows = lax.dynamic_slice_in_dim(own_keys, start, key_block, 0)
        value_rows = lax.dynamic_slice_in_dim(own_values, start, key_block, 0)
        prob_half, dscore = backward_block(
            query_rows, grad_rows, lse, delta, key_rows, value_rows, score_scale
        )
        qgrad_now = qgrad_now + jnp.dot(dscore, key_rows, preferred_element_type=jnp.float32)
        both = jnp.concatenate(
            [contract_cols(dscore, query_rows), contract_cols(prob_half, grad_rows)], 1
        )
        partial_grads = lax.dynamic_update_slice_in_dim(partial_grads, both, start, 0)
        return (qgrad_now, partial_grads)

    qgrad, partial_grads = lax.fori_loop(
        0, own_steps, own_backward, (qgrad, jnp.zeros((group_span, 2 * head_dim), jnp.float32))
    )
    summed = lax.psum_scatter(partial_grads, "seq", scatter_dimension=0, tiled=True)
    key_grad = summed[:, :head_dim]
    value_grad = summed[:, head_dim:]
    query_grad = qgrad.reshape(local_rows, width)
    return (gated_out, query_grad, key_grad, value_grad)


def solution(mesh):
    return jax.shard_map(
        body,
        mesh=mesh,
        in_specs=(
            P(("tm", "seq"), None),
            P(("tm", "seq"), None),
            P(("tm", "seq"), None),
            P(("tm", "seq"), None),
            P(("tm", "seq"), None),
            P("tm"),
            P(),
            P(("tm", "seq"), None),
        ),
        out_specs=(
            P(("tm", "seq"), None),
            P(("tm", "seq"), None),
            P(("tm", "seq"), None),
            P(("tm", "seq"), None),
        ),
        check_vma=False,
    )
```

profile of v0, /device:TPU:224, one launch (start us, length us, event | category | flops | bytes accessed | tf_op | source)
XLA Modules:
  0.0 667.8 jit_solution(3871034587657873193)
XLA Ops:
  12.6 116.4 %all-gather.5.cloned.1.call-done = bf16[32768,128]{1,0:T(8,128)(2,1)} async-done(((bf16[128,128]{1,0:T(8,128)(2,1)}), bf16[32768,128]{1,0:T(8,128)(2,1)}) %all-gather.5.cloned.1.call-update) | async-done | bytes 8388624 | tf_op jit(solution)/shard_map/all_gather | solution.py:53
  129.0 118.7 %all-gather.7.cloned.1.call-done = bf16[32768,128]{1,0:T(8,128)(2,1)} async-done(((bf16[128,128]{1,0:T(8,128)(2,1)}), bf16[32768,128]{1,0:T(8,128)(2,1)}) %all-gather.7.cloned.1.call-update) | async-done | bytes 8388624 | tf_op jit(solution)/shard_map/all_gather | solution.py:54
  247.8 94.3 %while.56 = (s32[]{:T(128)}, f32[512]{0:T(512)S(1)}, f32[512]{0:T(512)S(1)}, f32[512,128]{1,0:T(8,128)S(1)}, s32[]{:T(128)}, /*index=5*/bf16[32768,128]{1,0:T(8,...) while((s32[]{:T(128)}, f32[512]{0:T(512)S(1)}, ...), condition=%wide.region_3.0_spmd, body=%wide.region_0.0_spmd.sunk | while | flops 272761856 | bytes 7504043 | solution.py:84
  342.1 3.9 all-gather.11.cloned.1.call-done
  346.0 13.4 %while.57 = (s32[]{:T(128)}, f32[512]{0:T(512)S(1)}, f32[512]{0:T(512)S(1)}, f32[512,128]{1,0:T(8,128)S(1)}, bf16[4096,128]{1,0:T(8,128)(2,1)}, /*index=5*/bf16[...) while((s32[]{:T(128)}, f32[512]{0:T(512)S(1)}, ...), condition=%wide.region_7.0_spmd, body=%wide.region_4.0_spmd.sunk | while | flops 272761856 | bytes 7504035 | solution.py:85
  361.0 170.3 %while.58 = (s32[]{:T(128)}, f32[512,128]{1,0:T(8,128)}, s32[]{:T(128)}, bf16[32768,128]{1,0:T(8,128)(2,1)}, bf16[512,128]{1,0:T(8,128)(2,1)S(1)}, /*index=5*/f3...) while((s32[]{:T(128)}, f32[512,128]{1,0:T(8,128)}, ...), condition=%wide.region_10.0_spmd, body=%wide.region_9.0_spmd.sunk | while | flops 405864448 | bytes 5772463 | solution.py:102
  369.8 3.4 fusion.108
  375.9 3.4 fusion.108
  382.0 3.4 fusion.108
  388.1 3.4 fusion.108
  400.2 3.4 fusion.108
  406.3 3.4 fusion.108
  424.5 3.4 fusion.108
  430.6 3.4 fusion.108
  448.9 3.4 fusion.108
  455.0 3.4 fusion.108
  473.2 3.4 fusion.108
  479.3 3.4 fusion.108
  497.5 3.4 fusion.108
  503.6 3.4 fusion.108
  521.9 3.4 fusion.108
  527.9 3.4 fusion.108
  533.5 39.5 %while.59 = (s32[]{:T(128)}, f32[512,128]{1,0:T(8,128)}, f32[4096,256]{1,0:T(8,128)}, bf16[4096,128]{1,0:T(8,128)(2,1)}, bf16[512,128]{1,0:T(8,128)(2,1)S(1)}, /...) while((s32[]{:T(128)}, f32[512,128]{1,0:T(8,128)}, ...), condition=%wide.region_12.0_spmd, body=%wide.region_11.0_spmd.sunk | while | flops 676134912 | bytes 18618556 | solution.py:121
  576.5 83.3 %reduce-scatter.2.cloned.1.call-done = f32[128,256]{1,0:T(8,128)} async-done(((f32[4096,256]{1,0:T(8,128)}), f32[128,256]{1,0:T(8,128)}) %reduce-scatter.2.cloned.1.call-update) | async-done | bytes 131088 | tf_op jit(solution)/shard_map/reduce_scatter | solution.py:124
  (298 shorter events, 275.8 us)
Async XLA Ops:
  7.2 4.5 copy-start
  7.2 5.3 copy-start.2
  7.2 121.8 %all-gather.5.cloned.1.call-start = ((), (), s32[]{:S(2)}) async-start(), calls=%async_computation.1 | async-start | bytes 8421376 | tf_op jit(solution)/shard_map/all_gather | solution.py:53
  7.9 239.8 %all-gather.7.cloned.1.call-start = ((), (), s32[]{:S(2)}) async-start(), calls=%async_computation.2 | async-start | bytes 8421376 | tf_op jit(solution)/shard_map/all_gather | solution.py:54
  8.7 333.4 %all-gather.9.cloned.1.call-start = ((), (), s32[]{:S(2)}) async-start(), calls=%async_computation.3 | async-start | bytes 1081344 | tf_op jit(solution)/shard_map/all_gather | solution.py:49
  9.4 336.6 %all-gather.11.cloned.1.call-start = ((), (), s32[]{:S(2)}) async-start(), calls=%async_computation.4 | async-start | bytes 1081344 | tf_op jit(solution)/shard_map/all_gather | solution.py:50
  10.0 649.8 %reduce-scatter.2.cloned.1.call-start = ((), (), s32[]{:S(2)}) async-start(), calls=%async_computation.5 | async-start | bytes 4325376 | tf_op jit(solution)/shard_map/reduce_scatter | solution.py:124
  573.1 0.9 copy-start.1
Sparse Core Ops, SparseCore 0:
  11.7 117.1 all-gather.4
  132.7 114.9 all-gather.6
  250.3 46.0 all-gather.8
  298.8 47.1 all-gather.10
  573.2 86.4 reduce-scatter.1
where the time goes:
time: 675 us; the launch traced here: 668 us
  waiting for transfers between devices  325 us (48%)
  matrix products  289 us (43%)
  other arithmetic  19.3 us (3%)
  local copies, waits for them, and re-layouts  18.8 us (3%)
  between operations  14.5 us (2%)
    dot_general x68, matrix products, contract_rows(): lax.dot_general(left, right, (((1,), (1,)), ((), ())), preferred_element_...  133 us
    all_gather x1, waiting for transfers between devices, body(): lax.all_gather(clean_values, ('tm', 'seq'), axis=0, tiled=True)  119 us
    all_gather x1, waiting for transfers between devices, body(): lax.all_gather(clean_keys, ('tm', 'seq'), axis=0, tiled=True)  116 us
    dot_general x28, matrix products, past_backward(): return qgrad + jnp.dot(dscore, key_rows, preferred_element_type=jnp.float32)  94.3 us
    reduce_scatter x1, waiting for transfers between devices, body(): lax.psum_scatter(partial_grads, 'seq', scatter_dimension=0, tiled=True)  83.3 us
    dot_general x32, matrix products, attend_block(): jnp.dot(expo.astype(jnp.bfloat16), value_rows, preferred_element_type=jnp...  48.2 us
  transfers between devices with their start and end apart: 5, of which 4 were waited for; matrix products, arithmetic and copies ran while one was open for 15% of the time, Pallas kernels for 0%

commit v1 on v0

v1 whole, which is shorter than its diff:
```python
import math

import jax
import jax.numpy as jnp
from jax import lax
from jax.experimental import pallas as pl
from jax.experimental.pallas import tpu as pltpu
from jax.sharding import PartitionSpec as P

MESH = pl.DeviceIdType.MESH
HALF = jnp.bfloat16
FULL = jnp.float32
SIDE = 4
PLANES = 8
TOK = 128
HD = 128
HEADS = 4
ROWS = HEADS * TOK
BOTH = 2 * ROWS
CUT = TOK // 2
REGION = SIDE * SIDE * CUT
LINE = SIDE * CUT
BK = REGION // 2
LEAD1 = 6
LEAD2 = 4


def dot(a, b):
    return lax.dot_general(a, b, (((1,), (0,)), ((), ())), preferred_element_type=FULL)


def dot_tn(a, b):
    return lax.dot_general(a, b, (((0,), (0,)), ((), ())), preferred_element_type=FULL)


def fold(a, op):
    return op(a.reshape(a.shape[0] // 8, 8, a.shape[1]), axis=0)


def kernel(
    timestep, query, key_in, value_in, clean_keys, clean_values, mod_table, out_grad,
    gated, query_grad, key_grad, value_grad,
    kv, clean, table, qg, qg_sib, qt, gt, q_rows, g_rows,
    s_buf, e_buf, x_buf, m_buf, al_buf, l_buf, o1, o2,
    ml, ml_sib, o1_sib, o2_sib, stats, stats_sib,
    part, own_part, rs1, rs2_out, rs2,
    table_sem, core_send, core_recv, z_send, z_recv, s1_send, s1_recv, s2_send, s2_recv,
    rs1_send, rs1_recv, rs2_send, rs2_recv,
):
    scale = 1.0 / math.sqrt(HD)
    to_log2 = scale * math.log2(math.e)
    z = lax.axis_index("tm")
    seq = lax.axis_index("seq")
    core = lax.rem(seq, 2)
    y = lax.rem(seq // 2, SIDE)
    x = seq // (2 * SIDE)
    regions = 2 * (z + 1)

    def chip(dx, dy):
        px = lax.rem(x + dx, SIDE)
        py = lax.rem(y + dy, SIDE)
        return (z, (px * SIDE + py) * 2 + core)

    sibling = (z, (x * SIDE + y) * 2 + 1 - core)

    def plane(pz):
        return (pz, seq)

    def remote(src, dst, send, recv, device):
        return pltpu.make_async_remote_copy(
            src_ref=src, dst_ref=dst, send_sem=send, recv_sem=recv,
            device_id=device, device_id_type=MESH,
        )

    def along_line(r, d):
        p = lax.rem(r, 2)
        return chip((1 - p) * d, p * d)

    def across_lines(r, d):
        p = lax.rem(r, 2)
        return chip(p * d, (1 - p) * d)

    def place(r):
        p = lax.rem(r, 2)
        return p * x + (1 - p) * y, p * y + (1 - p) * x

    table_copy = pltpu.make_async_copy(mod_table, table, table_sem)
    table_copy.start()

    barrier = pltpu.get_barrier_semaphore()
    for d in range(1, SIDE):
        pl.semaphore_signal(barrier, inc=1, device_id=chip(d, 0), device_id_type=MESH)
        pl.semaphore_signal(barrier, inc=1, device_id=chip(0, d), device_id_type=MESH)
    for d in range(1, PLANES):
        pl.semaphore_signal(
            barrier, inc=1, device_id=plane(lax.rem(z + d, PLANES)), device_id_type=MESH
        )
    pl.semaphore_signal(barrier, inc=1, device_id=sibling, device_id_type=MESH)

    for p in range(2):
        u, v = place(p)
        start = pl.multiple_of(u * LINE + v * CUT, CUT)
        rows = pl.ds(p * CUT, CUT)
        kv[p, pl.ds(start, CUT), :HD] = value_in[rows, :]
        kv[p, pl.ds(start, CUT), HD:] = key_in[rows, :]
    clean[:, :HD] = clean_values[...]
    clean[:, HD:] = clean_keys[...]

    pl.semaphore_wait(barrier, 2 * (SIDE - 1) + PLANES)

    def stage1(r):
        u, v = place(r)
        piece = kv.at[r, pl.ds(pl.multiple_of(u * LINE + v * CUT, CUT), CUT)]
        for d in range(1, SIDE):
            remote(piece, piece, s1_send.at[r], s1_recv.at[r], along_line(r, d)).start()

    def wait_part(r, sem, keys, sending):
        block = kv.at[r, pl.ds(0, keys)]
        pltpu.make_async_copy(block, block, sem.at[r]).wait()

    def stage2(r):
        wait_part(r, s1_recv, (SIDE - 1) * CUT, False)
        u, _ = place(r)
        line = kv.at[r, pl.ds(pl.multiple_of(u * LINE, LINE), LINE)]
        for d in range(1, SIDE):
            remote(line, line, s2_send.at[r], s2_recv.at[r], across_lines(r, d)).start()

    def clean_copy(r, device):
        p = lax.rem(r, 2)
        u, v = place(r)
        return remote(
            clean.at[pl.ds(pl.multiple_of(p * CUT, CUT), CUT)],
            kv.at[r, pl.ds(pl.multiple_of(u * LINE + v * CUT, CUT), CUT)],
            z_send.at[r], z_recv.at[r], device,
        )

    def clean_stage1(r):
        clean_copy(r, plane(z)).wait_recv()
        stage1(r)

    def wait_region(r):
        wait_part(r, s2_recv, (SIDE - 1) * LINE, False)

    stage1(0)
    stage1(1)

    table_copy.wait()
    gain = table[pl.ds(timestep[0], 1), :]
    qg[0] = query[...]
    qg[1] = (gain * out_grad[...].astype(FULL)).astype(HALF)
    share_rows = remote(qg, qg_sib, core_send.at[0], core_recv.at[0], sibling)
    share_rows.start()

    def send_clean(d, carry):
        @pl.when(z + d < PLANES)
        def _():
            for p in range(2):
                clean_copy(2 * d + p, plane(lax.rem(z + d, PLANES))).start()
        return carry

    lax.fori_loop(1, PLANES, send_clean, 0)

    def lay_rows(source, at):
        for h in range(HEADS):
            cols = pl.ds(h * HD, HD)
            rows = pl.ds(at + h * TOK, TOK)
            q_head = source[0, :, cols]
            g_head = source[1, :, cols]
            q_rows[rows, :] = q_head
            g_rows[rows, :] = g_head
            qt[:, rows] = q_head.T
            gt[:, rows] = g_head.T

    lay_rows(qg, 0)
    stage2(0)
    stage2(1)
    share_rows.wait_recv()
    lay_rows(qg_sib, ROWS)

    def lead_stage1(r, carry):
        @pl.when(r < regions)
        def _():
            clean_stage1(r)
        return carry

    def lead_stage2(r, carry):
        @pl.when(r < regions)
        def _():
            stage2(r)
        return carry

    lax.fori_loop(2, LEAD1, lead_stage1, 0)

    l_buf[...] = jnp.zeros_like(l_buf)
    o1[...] = jnp.zeros_like(o1)
    o2[...] = jnp.zeros_like(o2)
    e_buf[1] = jnp.zeros_like(e_buf[1])
    x_buf[1] = jnp.zeros_like(x_buf[1])
    al_buf[...] = jnp.ones_like(al_buf)
    m_buf[...] = jnp.full_like(m_buf, -1e30)

    lax.fori_loop(2, LEAD2, lead_stage2, 0)

    def scores(r, at, parity, j):
        cols = pl.ds(j * ROWS, ROWS)
        s = dot(kv[r, pl.ds(at, BK), HD:], qt[:, cols])
        s_buf[1 - parity, :, cols] = s
        before = m_buf[parity, :, cols]
        top = jnp.max(fold(s, jnp.max), axis=0, keepdims=True) * to_log2
        after = jnp.maximum(before, top)
        m_buf[1 - parity, :, cols] = after
        al_buf[1 - parity, :, cols] = jnp.exp2(before - after)

    def weigh(r, at, parity, j):
        cols = pl.ds(j * ROWS, ROWS)
        e = jnp.exp2(s_buf[parity, :, cols] * to_log2 - m_buf[parity, :1, cols])
        dprob = dot(kv[r, pl.ds(at, BK), :HD], gt[:, cols])
        e_buf[parity, :, cols] = e.astype(HALF)
        x_buf[parity, :, cols] = (e * dprob).astype(HALF)
        l_buf[:, cols] = l_buf[:, cols] * al_buf[parity, :, cols] + fold(e, jnp.sum)

    def gather_sums(r, at, parity, j):
        cols = pl.ds(j * ROWS, ROWS)
        al = al_buf[parity, :1, cols]
        o1[j] = o1[j] * al + dot_tn(kv[r, pl.ds(at, BK), :], e_buf[parity, :, cols])
        o2[j] = o2[j] * al + dot_tn(kv[r, pl.ds(at, BK), HD:], x_buf[parity, :, cols])

    wait_region(0)
    for j in range(2):
        scores(0, 0, 1, j)

    def step(i, carry):
        @pl.when(i + LEAD1 < regions)
        def _():
            clean_stage1(i + LEAD1)

        @pl.when(i + LEAD2 < regions)
        def _():
            stage2(i + LEAD2)

        @pl.when(i + 1 < regions)
        def _():
            wait_region(i + 1)

        last = jnp.maximum(i - 1, 0)
        following = jnp.minimum(i + 1, regions - 1)
        for j in range(2):
            weigh(i, 0, 0, j)
            gather_sums(last, BK, 1, j)
            scores(i, BK, 0, j)
        for j in range(2):
            weigh(i, BK, 1, j)
            gather_sums(i, 0, 0, j)
            scores(following, 0, 1, j)
        return carry

    lax.fori_loop(0, regions, step, 0)
    for j in (1, 0):
        gather_sums(regions - 1, BK, 1, j)
        if j == 1:
            ml[0] = m_buf[1, :, ROWS:]
            ml[1] = l_buf[:, ROWS:]
            shares = [
                remote(ml, ml_sib, core_send.at[1], core_recv.at[1], sibling),
                remote(o1.at[1], o1_sib, core_send.at[2], core_recv.at[2], sibling),
                remote(o2.at[1], o2_sib, core_send.at[3], core_recv.at[3], sibling),
            ]
            for share in shares:
                share.start()

    for share in shares:
        share.wait_recv()
    peak_a = m_buf[1, :1, :ROWS]
    peak_b = ml_sib[0, :1, :]
    peak = jnp.maximum(peak_a, peak_b)
    part_a = jnp.exp2(peak_a - peak)
    part_b = jnp.exp2(peak_b - peak)
    total = part_a * jnp.sum(l_buf[:, :ROWS], axis=0, keepdims=True) + part_b * jnp.sum(
        ml_sib[1], axis=0, keepdims=True
    )
    part_a = part_a / total
    part_b = part_b / total
    attended = (o1[0, :HD, :] * part_a + o1_sib[:HD, :] * part_b).astype(HALF)
    delta = jnp.sum(gt[:, :ROWS].astype(FULL) * attended.astype(FULL), axis=0, keepdims=True)
    stats[0] = jnp.broadcast_to(peak + jnp.log2(total), (8, ROWS))
    stats[1] = jnp.broadcast_to(delta, (8, ROWS))
    share_stats = remote(stats, stats_sib, core_send.at[4], core_recv.at[4], sibling)
    share_stats.start()

    mean_key = o1[0, HD:, :] * part_a + o1_sib[HD:, :] * part_b
    qgrad = (o2[0] * part_a + o2_sib[...] * part_b - delta * mean_key) * scale
    attended = attended.astype(FULL)
    for h in range(HEADS):
        cols = slice(h * HD, (h + 1) * HD)
        gated[:, cols] = gain[:, cols] * attended[:, h * TOK : (h + 1) * TOK].T
        query_grad[:, cols] = qgrad[:, h * TOK : (h + 1) * TOK].T
    share_stats.wait_recv()

    def backward(p, line):
        block = kv[p, pl.ds(pl.multiple_of(line * LINE, LINE), LINE), :]
        lse = jnp.concatenate([stats[0, :1, :], stats_sib[0, :1, :]], axis=1)
        drop = jnp.concatenate([stats[1, :1, :], stats_sib[1, :1, :]], axis=1)
        prob = jnp.exp2(dot(block[:, HD:], qt[...]) * to_log2 - lse)
        dprob = dot(block[:, :HD], gt[...])
        dscore = (prob * (dprob - drop) * scale).astype(HALF)
        vgrad = dot(prob.astype(HALF), g_rows[...])
        kgrad = dot(dscore, q_rows[...])
        return vgrad, kgrad

    def part_copy(p, d):
        return remote(
            part.at[p, d - 1], rs1.at[p, d - 1],
            rs1_send.at[p, d - 1], rs1_recv.at[p, d - 1], across_lines(p, d),
        )

    for d in (2, 1, 3):
        for p in range(2):
            u, _ = place(p)
            vgrad, kgrad = backward(p, lax.rem(u + d, SIDE))
            part[p, d - 1, :, :HD] = vgrad.astype(HALF)
            part[p, d - 1, :, HD:] = kgrad.astype(HALF)
            part_copy(p, d).start()
    for p in range(2):
        u, _ = place(p)
        vgrad, kgrad = backward(p, u)
        own_part[p, :, :HD] = vgrad
        own_part[p, :, HD:] = kgrad

    def piece_copy(p, d):
        _, v = place(p)
        at = pl.multiple_of(lax.rem(v + d, SIDE) * CUT, CUT)
        return remote(
            rs2_out.at[p, pl.ds(at, CUT)], rs2.at[p, d - 1],
            rs2_send.at[p, d - 1], rs2_recv.at[p, d - 1], along_line(p, d),
        )

    for p in range(2):
        for d in range(1, SIDE):
            part_copy(p, d).wait_recv()
        own_part[p] = (
            own_part[p] + rs1[p, 0].astype(FULL) + rs1[p, 1].astype(FULL) + rs1[p, 2].astype(FULL)
        )
        rs2_out[p] = own_part[p].astype(HALF)
        for d in range(1, SIDE):
            piece_copy(p, d).start()
    for p in range(2):
        _, v = place(p)
        for d in range(1, SIDE):
            piece_copy(p, d).wait_recv()
        mine = own_part[p, pl.ds(pl.multiple_of(v * CUT, CUT), CUT), :]
        mine = mine + rs2[p, 0].astype(FULL) + rs2[p, 1].astype(FULL) + rs2[p, 2].astype(FULL)
        value_grad[pl.ds(p * CUT, CUT), :] = mine[:, :HD]
        key_grad[pl.ds(p * CUT, CUT), :] = mine[:, HD:]

    for copy in [share_rows, share_stats] + shares:
        copy.wait_send()
    for p in range(2):
        for d in range(1, SIDE):
            part_copy(p, d).wait_send()
            piece_copy(p, d).wait_send()

    def drain(r, carry):
        wait_part(r, s1_send, (SIDE - 1) * CUT, True)
        wait_part(r, s2_send, (SIDE - 1) * LINE, True)
        return carry

    lax.fori_loop(0, regions, drain, 0)

    def drain_clean(d, carry):
        @pl.when(z + d < PLANES)
        def _():
            for p in range(2):
                clean_copy(2 * d + p, plane(lax.rem(z + d, PLANES))).wait_send()
        return carry

    lax.fori_loop(1, PLANES, drain_clean, 0)


def body(query_in, key_in, value_in, clean_keys, clean_values, timestep, mod_table, out_grad):
    vmem = pl.BlockSpec(memory_space=pltpu.VMEM)
    dma = pltpu.SemaphoreType.DMA
    slots = 2 * PLANES
    return pl.pallas_call(
        kernel,
        name="attend",
        out_shape=[
            jax.ShapeDtypeStruct((TOK, HEADS * HD), FULL),
            jax.ShapeDtypeStruct((TOK, HEADS * HD), FULL),
            jax.ShapeDtypeStruct((TOK, HD), FULL),
            jax.ShapeDtypeStruct((TOK, HD), FULL),
        ],
        in_specs=[pl.BlockSpec(memory_space=pltpu.SMEM)]
        + [vmem] * 5
        + [pl.BlockSpec(memory_space=pl.ANY), vmem],
        out_specs=[vmem] * 4,
        scratch_shapes=[
            pltpu.VMEM((slots, REGION, 2 * HD), HALF),
            pltpu.VMEM((TOK, 2 * HD), HALF),
            pltpu.VMEM(mod_table.shape, FULL),
            pltpu.VMEM((2, TOK, HEADS * HD), HALF),
            pltpu.VMEM((2, TOK, HEADS * HD), HALF),
            pltpu.VMEM((HD, BOTH), HALF),
            pltpu.VMEM((HD, BOTH), HALF),
            pltpu.VMEM((BOTH, HD), HALF),
            pltpu.VMEM((BOTH, HD), HALF),
            pltpu.VMEM((2, BK, BOTH), FULL),
            pltpu.VMEM((2, BK, BOTH), HALF),
            pltpu.VMEM((2, BK, BOTH), HALF),
            pltpu.VMEM((2, 8, BOTH), FULL),
            pltpu.VMEM((2, 8, BOTH), FULL),
            pltpu.VMEM((8, BOTH), FULL),
            pltpu.VMEM((2, 2 * HD, ROWS), FULL),
            pltpu.VMEM((2, HD, ROWS), FULL),
            pltpu.VMEM((2, 8, ROWS), FULL),
            pltpu.VMEM((2, 8, ROWS), FULL),
            pltpu.VMEM((2 * HD, ROWS), FULL),
            pltpu.VMEM((HD, ROWS), FULL),
            pltpu.VMEM((2, 8, ROWS), FULL),
            pltpu.VMEM((2, 8, ROWS), FULL),
            pltpu.VMEM((2, SIDE - 1, LINE, 2 * HD), HALF),
            pltpu.VMEM((2, LINE, 2 * HD), FULL),
            pltpu.VMEM((2, SIDE - 1, LINE, 2 * HD), HALF),
            pltpu.VMEM((2, LINE, 2 * HD), HALF),
            pltpu.VMEM((2, SIDE - 1, CUT, 2 * HD), HALF),
            dma,
            dma((5,)), dma((5,)),
            dma((slots,)), dma((slots,)),
            dma((slots,)), dma((slots,)),
            dma((slots,)), dma((slots,)),
            dma((2, SIDE - 1)), dma((2, SIDE - 1)),
            dma((2, SIDE - 1)), dma((2, SIDE - 1)),
        ],
        compiler_params=pltpu.CompilerParams(
            collective_id=0, has_side_effects=True, vmem_limit_bytes=50 * 2**20
        ),
    )(timestep, query_in, key_in, value_in, clean_keys, clean_values, mod_table, out_grad)


def solution(mesh):
    assert mesh.shape["tm"] == PLANES and mesh.shape["seq"] == 2 * SIDE * SIDE
    split = P(("tm", "seq"), None)
    return jax.shard_map(
        body,
        mesh=mesh,
        in_specs=(split, split, split, split, split, P("tm"), P(), split),
        out_specs=(split, split, split, split),
        check_vma=False,
    )
```

time: 675 us -> 103 us (0.15)
  waiting for transfers between devices: 325 us -> 0 us
  matrix products: 289 us -> 0 us
  Pallas kernels: 0 us -> 92.1 us
  other arithmetic: 19.3 us -> 0 us
  between operations: 14.5 us -> 1.3 us
  local copies, waits for them, and re-layouts: 18.8 us -> 9.07 us
    dot_general x141 -> x0, matrix products: 289 us -> none  [the longest x68 133 us: contract_rows(): lax.dot_general(left, right, (((1,), (1,)), ((), ())), preferred_element_...]
    all_gather x4 -> x0, waiting for transfers between devices: 239 us -> none  [the longest x1 119 us: body(): lax.all_gather(clean_values, ('tm', 'seq'), axis=0, tiled=True)]
    pallas_call x0 -> x1, Pallas kernels: none -> 92.1 us  [body(): pl.pallas_call(kernel, name='attend', out_shape=[jax.ShapeDtypeStruct((TO...]
    reduce_scatter x1 -> x0, waiting for transfers between devices: 83.3 us -> none  [body(): lax.psum_scatter(partial_grads, 'seq', scatter_dimension=0, tiled=True)]
    reduce_sum x33 -> x0, other arithmetic: 13.7 us -> none  [the longest x32 12.8 us: attend_block(): total = decay * total + jnp.sum(expo, axis=1)]
    dynamic_update_slice x8 -> x0, local copies, waits for them, and re-layouts: 10.5 us -> none  [own_backward(): lax.dynamic_update_slice_in_dim(partial_grads, both, start, 0)]
    unnamed x6 -> x18, local copies, waits for them, and re-layouts: 0.94 us -> 9.07 us
  transfers between devices with their start and end apart: 5 -> 0, of which waited for: 4 -> 0; matrix products, arithmetic and copies ran while one was open for 15% -> 0% of each run, Pallas kernels for 0% -> 0%
where the time goes in v1:
time: 103 us; the launch traced here: 102 us
  Pallas kernels  92.1 us (89%)
  local copies, waits for them, and re-layouts  9.07 us (9%)
  between operations  1.3 us (1%)
    pallas_call x1, Pallas kernels, body(): pl.pallas_call(kernel, name='attend', out_shape=[jax.ShapeDtypeStruct((TO...  92.1 us
    unnamed x18, local copies, waits for them, and re-layouts  9.07 us

profile of v1, /device:TPU:224, one launch (start us, length us, event | category | flops | bytes accessed | tf_op | source)
XLA Modules:
  0.0 102.5 jit_solution(7912641946140641819)
XLA Ops:
  1.3 0.0 copy-start
  1.3 1.6 %copy-done = f32[1000,512]{1,0:T(8,128)S(1)} copy-done((f32[1000,512]{1,0:T(8,128)S(1)}, f32[1000,512]{1,0:T(8,128)}, u32[]{:S(2)}) %copy-start) | copy-done | bytes 2048024
  2.9 0.0 copy-start.1
  2.9 0.9 copy-done.1
  3.8 0.0 copy-start.2
  3.8 0.9 copy-done.2
  4.7 0.0 copy-start.3
  4.7 0.8 copy-done.3
  5.4 0.0 copy-start.4
  5.4 0.8 copy-done.4
  6.2 0.0 copy-start.5
  6.2 0.8 copy-done.5
  6.9 0.0 copy-start.6
  6.9 0.8 copy-done.6
  7.7 92.1 %attend.1 = (f32[128,512]{1,0:T(8,128)S(1)}, f32[128,512]{1,0:T(8,128)S(1)}, f32[128,128]{1,0:T(8,128)S(1)}, f32[128,128]{1,0:T(8,128)S(1)}) custom-call(s32[1]{0:T(128)S(6)} %copy.16.timestep, bf16[128,512]{1,0:T(8,128)(2,1)S(1)} %copy-done.1, bf16[128,128]{1,0:T(8,128)(2,1)S(1)} %copy-done.3, bf16[128,128]{1,0:T(8,128)(2,1)S(1)} %copy-done.4, ...), custom_call_target="tpu_custom_call" | custom-call | tf_op jit(solution)/shard_map/attend/pallas_call | solution.py:383
  99.8 0.7 copy.17
  100.5 0.7 copy.18
  101.2 0.6 copy.19
  101.8 0.6 copy.20
Async XLA Ops:
  1.3 1.6 %copy-start = (f32[1000,512]{1,0:T(8,128)S(1)}, f32[1000,512]{1,0:T(8,128)}, u32[]{:S(2)}) copy-start(f32[1000,512]{1,0:T(8,128)} %mod_table.1) | copy-start | bytes 6144004
  2.9 0.9 copy-start.1
  3.8 0.9 copy-start.2
  4.7 0.8 copy-start.3
  5.4 0.8 copy-start.4
  6.2 0.8 copy-start.5
  6.9 0.8 copy-start.6

commit v2 on v1

--- a/solution.py
+++ b/solution.py
@@ -21,8 +21,6 @@
 REGION = SIDE * SIDE * CUT
 LINE = SIDE * CUT
 BK = REGION // 2
-LEAD1 = 6
-LEAD2 = 4
 
 
 def dot(a, b):
@@ -40,11 +38,12 @@
 def kernel(
     timestep, query, key_in, value_in, clean_keys, clean_values, mod_table, out_grad,
     gated, query_grad, key_grad, value_grad,
-    kv, clean, table, qg, qg_sib, qt, gt, q_rows, g_rows,
+    kv, clean, table, grad_in, qg, qg_sib, qt, gt, q_rows, g_rows,
     s_buf, e_buf, x_buf, m_buf, al_buf, l_buf, o1, o2,
     ml, ml_sib, o1_sib, o2_sib, stats, stats_sib,
     part, own_part, rs1, rs2_out, rs2,
-    table_sem, core_send, core_recv, z_send, z_recv, s1_send, s1_recv, s2_send, s2_recv,
+    in_sem, core_send, core_recv, z_send, z_recv,
+    s1_send, s1_recv, up_send, up_recv, down_send, down_recv, s3_send, s3_recv,
     rs1_send, rs1_recv, rs2_send, rs2_recv,
 ):
     scale = 1.0 / math.sqrt(HD)
@@ -72,20 +71,42 @@
             device_id=device, device_id_type=MESH,
         )
 
-    def along_line(r, d):
-        p = lax.rem(r, 2)
+    def along_line(p, d):
         return chip((1 - p) * d, p * d)
 
-    def across_lines(r, d):
-        p = lax.rem(r, 2)
+    def across_lines(p, d):
         return chip(p * d, (1 - p) * d)
 
-    def place(r):
-        p = lax.rem(r, 2)
+    def place(p):
         return p * x + (1 - p) * y, p * y + (1 - p) * x
 
-    table_copy = pltpu.make_async_copy(mod_table, table, table_sem)
-    table_copy.start()
+    loads = [
+        pltpu.make_async_copy(query, qg.at[0], in_sem.at[0]),
+        pltpu.make_async_copy(out_grad, grad_in, in_sem.at[1]),
+        pltpu.make_async_copy(mod_table, table, in_sem.at[2]),
+    ]
+    shards = []
+    for p in range(2):
+        u, v = place(p)
+        rows = pl.ds(p * CUT, CUT)
+        noisy_at = pl.ds(pl.multiple_of(u * LINE + v * CUT, CUT), CUT)
+        for at, (noisy_in, clean_in) in enumerate(
+            ((value_in, clean_values), (key_in, clean_keys))
+        ):
+            cols = pl.ds(at * HD, HD)
+            sem = 3 + 4 * p + 2 * at
+            shards.append(
+                pltpu.make_async_copy(
+                    noisy_in.at[rows, :], kv.at[p, noisy_at, cols], in_sem.at[sem]
+                )
+            )
+            shards.append(
+                pltpu.make_async_copy(
+                    clean_in.at[rows, :], clean.at[p, :, cols], in_sem.at[sem + 1]
+                )
+            )
+    for load in shards + loads:
+        load.start()
 
     barrier = pltpu.get_barrier_semaphore()
     for d in range(1, SIDE):
@@ -96,69 +117,83 @@
             barrier, inc=1, device_id=plane(lax.rem(z + d, PLANES)), device_id_type=MESH
         )
     pl.semaphore_signal(barrier, inc=1, device_id=sibling, device_id_type=MESH)
-
-    for p in range(2):
-        u, v = place(p)
-        start = pl.multiple_of(u * LINE + v * CUT, CUT)
-        rows = pl.ds(p * CUT, CUT)
-        kv[p, pl.ds(start, CUT), :HD] = value_in[rows, :]
-        kv[p, pl.ds(start, CUT), HD:] = key_in[rows, :]
-    clean[:, :HD] = clean_values[...]
-    clean[:, HD:] = clean_keys[...]
-
+    for load in shards:
+        load.wait()
     pl.semaphore_wait(barrier, 2 * (SIDE - 1) + PLANES)
 
-    def stage1(r):
-        u, v = place(r)
-        piece = kv.at[r, pl.ds(pl.multiple_of(u * LINE + v * CUT, CUT), CUT)]
+    def arrived(block, sem):
+        pltpu.make_async_copy(block, block, sem).wait()
+
+    def piece_at(r):
+        u, v = place(lax.rem(r, 2))
+        return kv.at[r, pl.ds(pl.multiple_of(u * LINE + v * CUT, CUT), CUT)]
+
+    def gather_line(r):
+        piece = piece_at(r)
         for d in range(1, SIDE):
-            remote(piece, piece, s1_send.at[r], s1_recv.at[r], along_line(r, d)).start()
-
-    def wait_part(r, sem, keys, sending):
-        block = kv.at[r, pl.ds(0, keys)]
-        pltpu.make_async_copy(block, block, sem.at[r]).wait()
-
-    def stage2(r):
-        wait_part(r, s1_recv, (SIDE - 1) * CUT, False)
-        u, _ = place(r)
-        line = kv.at[r, pl.ds(pl.multiple_of(u * LINE, LINE), LINE)]
-        for d in range(1, SIDE):
-            remote(line, line, s2_send.at[r], s2_recv.at[r], across_lines(r, d)).start()
-
-    def clean_copy(r, device):
+            remote(
+                piece, piece, s1_send.at[r], s1_recv.at[r], along_line(lax.rem(r, 2), d)
+            ).start()
+
+    for p in range(2):
+        gather_line(p)
+
+    def line_at(r, shift):
+        u, _ = place(lax.rem(r, 2))
+        line = lax.rem(u + shift, SIDE)
+        return kv.at[r, pl.ds(pl.multiple_of(line * LINE, LINE), LINE)]
+
+    def half_line_at(r, shift, second):
+        u, _ = place(lax.rem(r, 2))
+        line = lax.rem(u + shift, SIDE)
+        return kv.at[r, pl.ds(pl.multiple_of(line * LINE + second * (LINE // 2), LINE // 2), LINE // 2)]
+
+    def spread(r):
         p = lax.rem(r, 2)
-        u, v = place(r)
+        line = line_at(r, 0)
+        remote(line, line, up_send.at[r], up_recv.at[r], across_lines(p, 1)).start()
+        remote(line, line, down_send.at[r], down_recv.at[r], across_lines(p, SIDE - 1)).start()
+
+    def pass_on(r):
+        p = lax.rem(r, 2)
+        arrived(line_at(r, SIDE - 1), up_recv.at[r])
+        first = half_line_at(r, SIDE - 1, 0)
+        remote(first, first, s3_send.at[r], s3_recv.at[r], across_lines(p, 1)).start()
+        arrived(line_at(r, 1), down_recv.at[r])
+        second = half_line_at(r, 1, 1)
+        remote(second, second, s3_send.at[r], s3_recv.at[r], across_lines(p, SIDE - 1)).start()
+
+    def complete(r):
+        arrived(line_at(r, 2), s3_recv.at[r])
+
+    def shard_copy(r):
         return remote(
-            clean.at[pl.ds(pl.multiple_of(p * CUT, CUT), CUT)],
-            kv.at[r, pl.ds(pl.multiple_of(u * LINE + v * CUT, CUT), CUT)],
-            z_send.at[r], z_recv.at[r], device,
+            clean.at[lax.rem(r, 2)], piece_at(r), z_send.at[r], z_recv.at[r],
+            plane(lax.rem(z + r // 2, PLANES)),
         )
 
-    def clean_stage1(r):
-        clean_copy(r, plane(z)).wait_recv()
-        stage1(r)
-
-    def wait_region(r):
-        wait_part(r, s2_recv, (SIDE - 1) * LINE, False)
-
-    stage1(0)
-    stage1(1)
-
-    table_copy.wait()
-    gain = table[pl.ds(timestep[0], 1), :]
-    qg[0] = query[...]
-    qg[1] = (gain * out_grad[...].astype(FULL)).astype(HALF)
-    share_rows = remote(qg, qg_sib, core_send.at[0], core_recv.at[0], sibling)
-    share_rows.start()
-
-    def send_clean(d, carry):
+    def send_shards(d, carry):
         @pl.when(z + d < PLANES)
         def _():
             for p in range(2):
-                clean_copy(2 * d + p, plane(lax.rem(z + d, PLANES))).start()
+                shard_copy(2 * d + p).start()
         return carry
 
-    lax.fori_loop(1, PLANES, send_clean, 0)
+    def take_shard(r):
+        arrived(piece_at(r), z_recv.at[r])
+        gather_line(r)
+
+    def take_line(r):
+        arrived(kv.at[r, pl.ds(0, (SIDE - 1) * CUT)], s1_recv.at[r])
+        spread(r)
+
+    lax.fori_loop(1, PLANES, send_shards, 0)
+    for load in loads:
+        load.wait()
+    gain = table[pl.ds(timestep[0], 1), :]
+    qg[1] = (gain * grad_in[...].astype(FULL)).astype(HALF)
+    share_rows = remote(qg, qg_sib, core_send.at[0], core_recv.at[0], sibling)
+    share_rows.start()
 
     def lay_rows(source, at):
         for h in range(HEADS):
@@ -172,24 +207,19 @@
             gt[:, rows] = g_head.T
 
     lay_rows(qg, 0)
-    stage2(0)
-    stage2(1)
+    for p in range(2):
+        take_line(p)
     share_rows.wait_recv()
     lay_rows(qg_sib, ROWS)
 
-    def lead_stage1(r, carry):
-        @pl.when(r < regions)
-        def _():
-            clean_stage1(r)
-        return carry
-
-    def lead_stage2(r, carry):
-        @pl.when(r < regions)
-        def _():
-            stage2(r)
-        return carry
-
-    lax.fori_loop(2, LEAD1, lead_stage1, 0)
+    def lead(low, high, work):
+        def one(r, carry):
+            @pl.when(r < regions)
+            def _():
+                work(r)
+            return carry
+
+        lax.fori_loop(low, high, one, 0)
 
     l_buf[...] = jnp.zeros_like(l_buf)
     o1[...] = jnp.zeros_like(o1)
@@ -199,11 +229,22 @@
     al_buf[...] = jnp.ones_like(al_buf)
     m_buf[...] = jnp.full_like(m_buf, -1e30)
 
-    lax.fori_loop(2, LEAD2, lead_stage2, 0)
-
-    def scores(r, at, parity, j):
+    def first_block(t):
+        i, h = t // 2, lax.rem(t, 2)
+        return (2 * i + h, h), (2 * i + 1, 3 * h)
+
+    def second_block(t):
+        i, h = t // 2, lax.rem(t, 2)
+        return (2 * i, 1 + h), (2 * i + h, 3 - h)
+
+    def rows_of(block, cols):
+        return jnp.concatenate([line_at(r, shift)[:, cols] for r, shift in block], axis=0)
+
+    values, keys, all_cols = slice(0, HD), slice(HD, 2 * HD), slice(0, 2 * HD)
+
+    def scores(block, parity, j):
         cols = pl.ds(j * ROWS, ROWS)
-        s = dot(kv[r, pl.ds(at, BK), HD:], qt[:, cols])
+        s = dot(rows_of(block, keys), qt[:, cols])
         s_buf[1 - parity, :, cols] = s
         before = m_buf[parity, :, cols]
         top = jnp.max(fold(s, jnp.max), axis=0, keepdims=True) * to_log2
@@ -211,52 +252,67 @@
         m_buf[1 - parity, :, cols] = after
         al_buf[1 - parity, :, cols] = jnp.exp2(before - after)
 
-    def weigh(r, at, parity, j):
+    def weigh(block, parity, j):
         cols = pl.ds(j * ROWS, ROWS)
         e = jnp.exp2(s_buf[parity, :, cols] * to_log2 - m_buf[parity, :1, cols])
-        dprob = dot(kv[r, pl.ds(at, BK), :HD], gt[:, cols])
+        dprob = dot(rows_of(block, values), gt[:, cols])
         e_buf[parity, :, cols] = e.astype(HALF)
         x_buf[parity, :, cols] = (e * dprob).astype(HALF)
         l_buf[:, cols] = l_buf[:, cols] * al_buf[parity, :, cols] + fold(e, jnp.sum)
 
-    def gather_sums(r, at, parity, j):
+    def gather_sums(block, parity, j):
         cols = pl.ds(j * ROWS, ROWS)
         al = al_buf[parity, :1, cols]
-        o1[j] = o1[j] * al + dot_tn(kv[r, pl.ds(at, BK), :], e_buf[parity, :, cols])
-        o2[j] = o2[j] * al + dot_tn(kv[r, pl.ds(at, BK), HD:], x_buf[parity, :, cols])
-
-    wait_region(0)
+        o1[j] = o1[j] * al + dot_tn(rows_of(block, all_cols), e_buf[parity, :, cols])
+        o2[j] = o2[j] * al + dot_tn(rows_of(block, keys), x_buf[parity, :, cols])
+
+    def half_step(t, h, j):
+        if h == 0:
+            weigh(first_block(t), 0, j)
+            gather_sums(second_block(jnp.maximum(t - 1, 0)), 1, j)
+            scores(second_block(t), 0, j)
+        else:
+            weigh(second_block(t), 1, j)
+            gather_sums(first_block(t), 0, j)
+            scores(first_block(jnp.minimum(t + 1, regions - 1)), 1, j)
+
+    def finish_unit(t):
+        @pl.when(lax.rem(t, 2) == 1)
+        def _():
+            complete(t - 1)
+            complete(t)
+
+    lead(2, 6, take_shard)
     for j in range(2):
-        scores(0, 0, 1, j)
-
-    def step(i, carry):
-        @pl.when(i + LEAD1 < regions)
-        def _():
-            clean_stage1(i + LEAD1)
-
-        @pl.when(i + LEAD2 < regions)
-        def _():
-            stage2(i + LEAD2)
-
-        @pl.when(i + 1 < regions)
-        def _():
-            wait_region(i + 1)
-
-        last = jnp.maximum(i - 1, 0)
-        following = jnp.minimum(i + 1, regions - 1)
+        scores(first_block(0), 1, j)
+    for p in range(2):
+        pass_on(p)
+    lead(2, 4, take_line)
+
+    def step(t, carry):
+        finish_unit(t)
         for j in range(2):
-            weigh(i, 0, 0, j)
-            gather_sums(last, BK, 1, j)
-            scores(i, BK, 0, j)
+            half_step(t, 0, j)
+        lead(t + 8 - 2 * jnp.maximum(1 - t, 0), t + 9, take_shard)
+        lead(jnp.minimum(2 * t + 4, t + 6), jnp.minimum(2 * t + 6, t + 7), take_line)
+        lead(jnp.maximum(jnp.minimum(2 * t, t + 3), 2), jnp.minimum(2 * t + 2, t + 4), pass_on)
         for j in range(2):
-            weigh(i, BK, 1, j)
-            gather_sums(i, 0, 0, j)
-            scores(following, 0, 1, j)
+            half_step(t, 1, j)
         return carry
 
-    lax.fori_loop(0, regions, step, 0)
+    lax.fori_loop(0, regions - 2, step, 0)
+
     for j in (1, 0):
-        gather_sums(regions - 1, BK, 1, j)
+
+        def last_step(t, carry):
+            if j == 1:
+                finish_unit(t)
+            half_step(t, 0, j)
+            half_step(t, 1, j)
+            return carry
+
+        lax.fori_loop(regions - 2, regions, last_step, 0)
+        gather_sums(second_block(regions - 1), 1, j)
         if j == 1:
             ml[0] = m_buf[1, :, ROWS:]
             ml[1] = l_buf[:, ROWS:]
@@ -294,18 +350,25 @@
         cols = slice(h * HD, (h + 1) * HD)
         gated[:, cols] = gain[:, cols] * attended[:, h * TOK : (h + 1) * TOK].T
         query_grad[:, cols] = qgrad[:, h * TOK : (h + 1) * TOK].T
-    share_stats.wait_recv()
-
-    def backward(p, line):
+    def backward(p, line, cols, lse, drop):
         block = kv[p, pl.ds(pl.multiple_of(line * LINE, LINE), LINE), :]
+        prob = jnp.exp2(dot(block[:, HD:], qt[:, cols]) * to_log2 - lse)
+        dprob = dot(block[:, :HD], gt[:, cols])
+        dscore = (prob * (dprob - drop) * scale).astype(HALF)
+        vgrad = dot(prob.astype(HALF), g_rows[cols, :])
+        kgrad = dot(dscore, q_rows[cols, :])
+        return vgrad, kgrad
+
+    def backward_mine(p, line):
+        return backward(p, line, pl.ds(0, ROWS), stats[0, :1, :], stats[1, :1, :])
+
+    def backward_theirs(p, line):
+        return backward(p, line, pl.ds(ROWS, ROWS), stats_sib[0, :1, :], stats_sib[1, :1, :])
+
+    def backward_all(p, line):
         lse = jnp.concatenate([stats[0, :1, :], stats_sib[0, :1, :]], axis=1)
         drop = jnp.concatenate([stats[1, :1, :], stats_sib[1, :1, :]], axis=1)
-        prob = jnp.exp2(dot(block[:, HD:], qt[...]) * to_log2 - lse)
-        dprob = dot(block[:, :HD], gt[...])
-        dscore = (prob * (dprob - drop) * scale).astype(HALF)
-        vgrad = dot(prob.astype(HALF), g_rows[...])
-        kgrad = dot(dscore, q_rows[...])
-        return vgrad, kgrad
+        return backward(p, line, pl.ds(0, BOTH), lse, drop)
 
     def part_copy(p, d):
         return remote(
@@ -313,16 +376,22 @@
             rs1_send.at[p, d - 1], rs1_recv.at[p, d - 1], across_lines(p, d),
         )
 
+    early = [backward_mine(p, lax.rem(place(p)[0] + 2, SIDE)) for p in range(2)]
+    share_stats.wait_recv()
     for d in (2, 1, 3):
         for p in range(2):
-            u, _ = place(p)
-            vgrad, kgrad = backward(p, lax.rem(u + d, SIDE))
+            line = lax.rem(place(p)[0] + d, SIDE)
+            if d == 2:
+                late = backward_theirs(p, line)
+                vgrad, kgrad = early[p][0] + late[0], early[p][1] + late[1]
+            else:
+                vgrad, kgrad = backward_all(p, line)
             part[p, d - 1, :, :HD] = vgrad.astype(HALF)
             part[p, d - 1, :, HD:] = kgrad.astype(HALF)
             part_copy(p, d).start()
     for p in range(2):
         u, _ = place(p)
-        vgrad, kgrad = backward(p, u)
+        vgrad, kgrad = backward_all(p, u)
         own_part[p, :, :HD] = vgrad
         own_part[p, :, HD:] = kgrad
 
@@ -360,20 +429,22 @@
             piece_copy(p, d).wait_send()
 
     def drain(r, carry):
-        wait_part(r, s1_send, (SIDE - 1) * CUT, True)
-        wait_part(r, s2_send, (SIDE - 1) * LINE, True)
+        line = line_at(r, 0)
+        for sem in (up_send, down_send, s3_send):
+            arrived(line, sem.at[r])
+        arrived(kv.at[r, pl.ds(0, (SIDE - 1) * CUT)], s1_send.at[r])
         return carry
 
     lax.fori_loop(0, regions, drain, 0)
 
-    def drain_clean(d, carry):
+    def drain_shards(d, carry):
         @pl.when(z + d < PLANES)
         def _():
             for p in range(2):
-                clean_copy(2 * d + p, plane(lax.rem(z + d, PLANES))).wait_send()
+                shard_copy(2 * d + p).wait_send()
         return carry
 
-    lax.fori_loop(1, PLANES, drain_clean, 0)
+    lax.fori_loop(1, PLANES, drain_shards, 0)
 
 
 def body(query_in, key_in, value_in, clean_keys, clean_values, timestep, mod_table, out_grad):
@@ -390,13 +461,13 @@
             jax.ShapeDtypeStruct((TOK, HD), FULL),
         ],
         in_specs=[pl.BlockSpec(memory_space=pltpu.SMEM)]
-        + [vmem] * 5
-        + [pl.BlockSpec(memory_space=pl.ANY), vmem],
+        + [pl.BlockSpec(memory_space=pl.ANY)] * 7,
         out_specs=[vmem] * 4,
         scratch_shapes=[
             pltpu.VMEM((slots, REGION, 2 * HD), HALF),
-            pltpu.VMEM((TOK, 2 * HD), HALF),
+            pltpu.VMEM((2, CUT, 2 * HD), HALF),
             pltpu.VMEM(mod_table.shape, FULL),
+            pltpu.VMEM((TOK, HEADS * HD), HALF),
             pltpu.VMEM((2, TOK, HEADS * HD), HALF),
             pltpu.VMEM((2, TOK, HEADS * HD), HALF),
             pltpu.VMEM((HD, BOTH), HALF),
@@ -422,8 +493,10 @@
             pltpu.VMEM((2, SIDE - 1, LINE, 2 * HD), HALF),
             pltpu.VMEM((2, LINE, 2 * HD), HALF),
             pltpu.VMEM((2, SIDE - 1, CUT, 2 * HD), HALF),
-            dma,
+            dma((11,)),
             dma((5,)), dma((5,)),
+            dma((slots,)), dma((slots,)),
+            dma((slots,)), dma((slots,)),
             dma((slots,)), dma((slots,)),
             dma((slots,)), dma((slots,)),
             dma((slots,)), dma((slots,)),
@@ -431,7 +504,7 @@
             dma((2, SIDE - 1)), dma((2, SIDE - 1)),
         ],
         compiler_params=pltpu.CompilerParams(
-            collective_id=0, has_side_effects=True, vmem_limit_bytes=50 * 2**20
+            collective_id=0, has_side_effects=True, vmem_limit_bytes=60 * 2**20
         ),
     )(timestep, query_in, key_in, value_in, clean_keys, clean_values, mod_table, out_grad)
 

time: 103 us -> 92.6 us (0.90)
  Pallas kernels: 92.1 us -> 84.7 us
  local copies, waits for them, and re-layouts: 9.07 us -> 6.29 us
    pallas_call x1, Pallas kernels: 92.1 us -> 84.7 us  [body(): pl.pallas_call(kernel, name='attend', out_shape=[jax.ShapeDtypeStruct((TO...]
    unnamed x18 -> x4, local copies, waits for them, and re-layouts: 9.07 us -> 6.29 us
where the time goes in v2:
time: 92.6 us; the launch traced here: 92.2 us
  Pallas kernels  84.7 us (91%)
  local copies, waits for them, and re-layouts  6.29 us (7%)
  between operations  1.29 us (1%)
    pallas_call x1, Pallas kernels, body(): pl.pallas_call(kernel, name='attend', out_shape=[jax.ShapeDtypeStruct((TO...  84.7 us
    unnamed x4, local copies, waits for them, and re-layouts  6.29 us

profile of v2, /device:TPU:224, one launch (start us, length us, event | category | flops | bytes accessed | tf_op | source)
XLA Modules:
  0.0 92.2 jit_solution(16420400950688993549)
XLA Ops:
  1.3 84.7 %attend.1 = (f32[128,512]{1,0:T(8,128)}, f32[128,512]{1,0:T(8,128)}, f32[128,128]{1,0:T(8,128)}, f32[128,128]{1,0:T(8,128)}) custom-call(s32[1]{0:T(128)S(6)} %copy.16.timestep, bf16[128,512]{1,0:T(8,128)(2,1)} %query.1, bf16[128,128]{1,0:T(8,128)(2,1)} %key_in.1, bf16[128,128]{1,0:T(8,128)(2,1)} %value_in.1, bf16[128,128]{1,0:T(8,128)(2,1)} %clean_keys.1, ...), custom_call_target="tpu_custom_call" | custom-call | tf_op jit(solution)/shard_map/attend/pallas_call | solution.py:454
  86.0 1.7 %copy.17 = f32[128,512]{1,0:T(8,128)} copy(f32[128,512]{1,0:T(8,128)} %get-tuple-element.8) | data formatting | bytes 524288
  87.6 1.7 %copy.18 = f32[128,512]{1,0:T(8,128)} copy(f32[128,512]{1,0:T(8,128)} %get-tuple-element.9) | data formatting | bytes 524288
  89.3 1.5 %copy.19 = f32[128,128]{1,0:T(8,128)} copy(f32[128,128]{1,0:T(8,128)} %get-tuple-element.10) | data formatting | bytes 131072
  90.8 1.5 %copy.20 = f32[128,128]{1,0:T(8,128)} copy(f32[128,128]{1,0:T(8,128)} %get-tuple-element.11) | data formatting | bytes 131072

commit v3 on v2

--- a/solution.py
+++ b/solution.py
@@ -21,6 +21,7 @@
 REGION = SIDE * SIDE * CUT
 LINE = SIDE * CUT
 BK = REGION // 2
+MOVED = 3
 
 
 def dot(a, b):
@@ -38,11 +39,11 @@
 def kernel(
     timestep, query, key_in, value_in, clean_keys, clean_values, mod_table, out_grad,
     gated, query_grad, key_grad, value_grad,
-    kv, clean, table, grad_in, qg, qg_sib, qt, gt, q_rows, g_rows,
-    s_buf, e_buf, x_buf, m_buf, al_buf, l_buf, o1, o2,
-    ml, ml_sib, o1_sib, o2_sib, stats, stats_sib,
+    kv, clean, table, grad_in, qg, qg_sib, qg_far, qg_far_sib, qt, gt, q_rows, g_rows,
+    s_buf, e_buf, x_buf, m_buf, al_buf, l_buf, m_own, o1, o2,
+    ml, ml_sib, o1_sib, o2_sib, far, far_lse, far_out, far_lse_out, stats, stats_sib,
     part, own_part, rs1, rs2_out, rs2,
-    in_sem, core_send, core_recv, z_send, z_recv,
+    in_sem, core_send, core_recv, far_send, far_recv, z_send, z_recv,
     s1_send, s1_recv, up_send, up_recv, down_send, down_recv, s3_send, s3_recv,
     rs1_send, rs1_recv, rs2_send, rs2_recv,
 ):
@@ -53,7 +54,20 @@
     core = lax.rem(seq, 2)
     y = lax.rem(seq // 2, SIDE)
     x = seq // (2 * SIDE)
-    regions = 2 * (z + 1)
+    helper, helped = z < MOVED, z > PLANES - 1 - MOVED
+    partner = (PLANES - 1 - z, seq)
+    own_units = jnp.minimum(z, PLANES - 1 - MOVED) + 1
+    helped_units = jnp.maximum(MOVED - z, 0)
+    gathered = 2 * (own_units + jnp.maximum(MOVED - 2 * z, 0))
+    rising = 1 - jnp.minimum(z // 2, 1)
+    first_plane = 1 - jnp.minimum(z, 1)
+
+    def region(order):
+        i = order // 2
+        falling = jnp.minimum(i, 1) * (z + 1 - i)
+        ahead = lax.rem(i + first_plane, gathered // 2)
+        return 2 * (rising * ahead + (1 - rising) * falling) + lax.rem(order, 2)
+
 
     def chip(dx, dy):
         px = lax.rem(x + dx, SIDE)
@@ -135,8 +149,16 @@
                 piece, piece, s1_send.at[r], s1_recv.at[r], along_line(lax.rem(r, 2), d)
             ).start()
 
+    @pl.when(2 * z < MOVED)
+    def _():
+        for p in range(2):
+            r = 2 * jnp.minimum(z + 1, MOVED) + p
+            u, v = place(p)
+            at = pl.ds(pl.multiple_of(u * LINE + v * CUT, CUT), CUT)
+            kv[r, at, :] = clean[p]
+
     for p in range(2):
-        gather_line(p)
+        gather_line(region(p))
 
     def line_at(r, shift):
         u, _ = place(lax.rem(r, 2))
@@ -166,85 +188,110 @@
     def complete(r):
         arrived(line_at(r, 2), s3_recv.at[r])
 
-    def shard_copy(r):
+    def shard_copy(p, d, pz):
         return remote(
-            clean.at[lax.rem(r, 2)], piece_at(r), z_send.at[r], z_recv.at[r],
-            plane(lax.rem(z + r // 2, PLANES)),
+            clean.at[p], piece_at(2 * jnp.minimum(z + 1, PLANES - 1) + p),
+            z_send.at[2 * d + p], z_recv.at[2 * jnp.minimum(z + 1, PLANES - 1) + p], plane(pz),
         )
 
-    def send_shards(d, carry):
-        @pl.when(z + d < PLANES)
+    def each_shard(low, high, act):
+        def one(d, carry):
+            @pl.when(z + d < PLANES)
+            def _():
+                for p in range(2):
+                    act(shard_copy(p, d, lax.rem(z + d, PLANES)))
+            return carry
+
+        lax.fori_loop(low, high, one, 0)
+
+    def left_shard(act):
+        @pl.when((z > 0) & (z < MOVED))
         def _():
             for p in range(2):
-                shard_copy(2 * d + p).start()
-        return carry
+                act(shard_copy(p, 0, 0))
+
+    def start(copy):
+        copy.start()
+
+    def wait_send(copy):
+        copy.wait_send()
 
     def take_shard(r):
-        arrived(piece_at(r), z_recv.at[r])
+        @pl.when((r > 1) & (r // 2 != z + 1))
+        def _():
+            arrived(piece_at(r), z_recv.at[r])
         gather_line(r)
 
     def take_line(r):
         arrived(kv.at[r, pl.ds(0, (SIDE - 1) * CUT)], s1_recv.at[r])
         spread(r)
 
-    lax.fori_loop(1, PLANES, send_shards, 0)
+    each_shard(1, 2, start)
+    left_shard(start)
+
     for load in loads:
         load.wait()
     gain = table[pl.ds(timestep[0], 1), :]
     qg[1] = (gain * grad_in[...].astype(FULL)).astype(HALF)
     share_rows = remote(qg, qg_sib, core_send.at[0], core_recv.at[0], sibling)
     share_rows.start()
-
-    def lay_rows(source, at):
+    far_rows = remote(qg, qg_far, far_send.at[0], far_recv.at[0], partner)
+    pass_rows = remote(qg_far, qg_far_sib, core_send.at[2], core_recv.at[2], sibling)
+
+    @pl.when(z == PLANES - 1)
+    def _():
+        far_rows.start()
+
+    def pass_far_rows():
+        far_rows.wait_recv()
+        pass_rows.start()
+
+
+    def lay_rows(source, task, at):
         for h in range(HEADS):
             cols = pl.ds(h * HD, HD)
             rows = pl.ds(at + h * TOK, TOK)
             q_head = source[0, :, cols]
             g_head = source[1, :, cols]
-            q_rows[rows, :] = q_head
-            g_rows[rows, :] = g_head
-            qt[:, rows] = q_head.T
-            gt[:, rows] = g_head.T
-
-    lay_rows(qg, 0)
+            if task == 0:
+                q_rows[rows, :] = q_head
+                g_rows[rows, :] = g_head
+            qt[task, :, rows] = q_head.T
+            gt[task, :, rows] = g_head.T
+
+    each_shard(2, 3, start)
+    lay_rows(qg, 0, 0)
     for p in range(2):
-        take_line(p)
+        take_line(region(p))
+    each_shard(3, 4, start)
     share_rows.wait_recv()
-    lay_rows(qg_sib, ROWS)
+    lay_rows(qg_sib, 0, ROWS)
 
     def lead(low, high, work):
-        def one(r, carry):
-            @pl.when(r < regions)
+        def one(order, carry):
+            @pl.when(order < gathered)
             def _():
-                work(r)
+                work(region(order))
             return carry
 
         lax.fori_loop(low, high, one, 0)
 
-    l_buf[...] = jnp.zeros_like(l_buf)
-    o1[...] = jnp.zeros_like(o1)
-    o2[...] = jnp.zeros_like(o2)
-    e_buf[1] = jnp.zeros_like(e_buf[1])
-    x_buf[1] = jnp.zeros_like(x_buf[1])
-    al_buf[...] = jnp.ones_like(al_buf)
-    m_buf[...] = jnp.full_like(m_buf, -1e30)
-
     def first_block(t):
-        i, h = t // 2, lax.rem(t, 2)
-        return (2 * i + h, h), (2 * i + 1, 3 * h)
+        r, h = region(t - lax.rem(t, 2)), lax.rem(t, 2)
+        return (r + h, h), (r + 1, 3 * h)
 
     def second_block(t):
-        i, h = t // 2, lax.rem(t, 2)
-        return (2 * i, 1 + h), (2 * i + h, 3 - h)
+        r, h = region(t - lax.rem(t, 2)), lax.rem(t, 2)
+        return (r, 1 + h), (r + h, 3 - h)
 
     def rows_of(block, cols):
         return jnp.concatenate([line_at(r, shift)[:, cols] for r, shift in block], axis=0)
 
     values, keys, all_cols = slice(0, HD), slice(HD, 2 * HD), slice(0, 2 * HD)
 
-    def scores(block, parity, j):
+    def scores(task, block, parity, j):
         cols = pl.ds(j * ROWS, ROWS)
-        s = dot(rows_of(block, keys), qt[:, cols])
+        s = dot(rows_of(block, keys), qt[task, :, cols])
         s_buf[1 - parity, :, cols] = s
         before = m_buf[parity, :, cols]
         top = jnp.max(fold(s, jnp.max), axis=0, keepdims=True) * to_log2
@@ -252,108 +299,215 @@
         m_buf[1 - parity, :, cols] = after
         al_buf[1 - parity, :, cols] = jnp.exp2(before - after)
 
-    def weigh(block, parity, j):
+    def weigh(task, block, parity, j):
         cols = pl.ds(j * ROWS, ROWS)
         e = jnp.exp2(s_buf[parity, :, cols] * to_log2 - m_buf[parity, :1, cols])
-        dprob = dot(rows_of(block, values), gt[:, cols])
+        dprob = dot(rows_of(block, values), gt[task, :, cols])
         e_buf[parity, :, cols] = e.astype(HALF)
         x_buf[parity, :, cols] = (e * dprob).astype(HALF)
-        l_buf[:, cols] = l_buf[:, cols] * al_buf[parity, :, cols] + fold(e, jnp.sum)
-
-    def gather_sums(block, parity, j):
+        l_buf[task, :, cols] = l_buf[task, :, cols] * al_buf[parity, :, cols] + fold(e, jnp.sum)
+
+    def gather_sums(task, block, parity, j):
         cols = pl.ds(j * ROWS, ROWS)
         al = al_buf[parity, :1, cols]
-        o1[j] = o1[j] * al + dot_tn(rows_of(block, all_cols), e_buf[parity, :, cols])
-        o2[j] = o2[j] * al + dot_tn(rows_of(block, keys), x_buf[parity, :, cols])
-
-    def half_step(t, h, j):
-        if h == 0:
-            weigh(first_block(t), 0, j)
-            gather_sums(second_block(jnp.maximum(t - 1, 0)), 1, j)
-            scores(second_block(t), 0, j)
-        else:
-            weigh(second_block(t), 1, j)
-            gather_sums(first_block(t), 0, j)
-            scores(first_block(jnp.minimum(t + 1, regions - 1)), 1, j)
-
-    def finish_unit(t):
-        @pl.when(lax.rem(t, 2) == 1)
+        o1[task, j] = o1[task, j] * al + dot_tn(rows_of(block, all_cols), e_buf[parity, :, cols])
+        o2[task, j] = o2[task, j] * al + dot_tn(rows_of(block, keys), x_buf[parity, :, cols])
+
+    def share_sums(task):
+        sem = 3 + 4 * task
+        pairs = (
+            (ml.at[task], ml_sib.at[task]),
+            (o1.at[task, 1, pl.ds(0, HD)], o1_sib.at[task, pl.ds(0, HD)]),
+            (o1.at[task, 1, pl.ds(HD, HD)], o1_sib.at[task, pl.ds(HD, HD)]),
+            (o2.at[task, 1], o2_sib.at[task]),
+        )
+        return [
+            remote(src, dst, core_send.at[sem + n], core_recv.at[sem + n], sibling)
+            for n, (src, dst) in enumerate(pairs)
+        ]
+
+    def both_cores(task):
+        for share in share_sums(task)[:2]:
+            share.wait_recv()
+        peak_a = m_own[task, :1, :]
+        peak_b = ml_sib[task, 0, :1, :]
+        peak = jnp.maximum(peak_a, peak_b)
+        part_a = jnp.exp2(peak_a - peak)
+        part_b = jnp.exp2(peak_b - peak)
+        total = part_a * jnp.sum(l_buf[task, :, :ROWS], axis=0, keepdims=True) + part_b * jnp.sum(
+            ml_sib[task, 1], axis=0, keepdims=True
+        )
+        return peak, total, part_a / total, part_b / total
+
+    far_sums = [
+        remote(far_lse_out, far_lse, far_send.at[1], far_recv.at[1], partner),
+        remote(
+            far_out.at[pl.ds(0, HD)], far.at[pl.ds(0, HD)], far_send.at[2], far_recv.at[2], partner
+        ),
+        remote(
+            far_out.at[pl.ds(HD, 2 * HD)], far.at[pl.ds(HD, 2 * HD)],
+            far_send.at[3], far_recv.at[3], partner,
+        ),
+    ]
+
+    def run(turn, carry):
+        task = first_plane * (1 - turn) + (1 - first_plane) * turn
+        begin = turn * 2 * (first_plane * MOVED + (1 - first_plane) * own_units)
+        first = 2 * (first_plane * (1 - task) * MOVED + (1 - first_plane) * task * jnp.maximum(z, 1))
+        end = first + (1 - task) * 2 * own_units + task * 2 * helped_units
+
+        l_buf[task] = jnp.zeros_like(l_buf[task])
+        o1[task] = jnp.zeros_like(o1[task])
+        o2[task] = jnp.zeros_like(o2[task])
+        e_buf[1] = jnp.zeros_like(e_buf[1])
+        x_buf[1] = jnp.zeros_like(x_buf[1])
+        al_buf[...] = jnp.ones_like(al_buf)
+        m_buf[...] = jnp.full_like(m_buf, -1e30)
+
+        def start_gathers():
+            for p in range(2):
+                pass_on(region(p))
+            each_shard(4, PLANES - MOVED, start)
+
+            @pl.when(helped & (z < PLANES - 1))
+            def _():
+                far_rows.start()
+
+            lead(2, 4, take_line)
+
+        @pl.when(turn == 0)
         def _():
-            complete(t - 1)
-            complete(t)
-
-    lead(2, 6, take_shard)
-    for j in range(2):
-        scores(first_block(0), 1, j)
-    for p in range(2):
-        pass_on(p)
-    lead(2, 4, take_line)
-
-    def step(t, carry):
-        finish_unit(t)
+            lead(2, 6, take_shard)
+
+            @pl.when(z == 0)
+            def _():
+                start_gathers()
+                pass_far_rows()
+
+        @pl.when(task == 1)
+        def _():
+            lay_rows(qg_far, 1, 0)
+            pass_rows.wait_recv()
+            lay_rows(qg_far_sib, 1, ROWS)
+
         for j in range(2):
-            half_step(t, 0, j)
-        lead(t + 8 - 2 * jnp.maximum(1 - t, 0), t + 9, take_shard)
-        lead(jnp.minimum(2 * t + 4, t + 6), jnp.minimum(2 * t + 6, t + 7), take_line)
-        lead(jnp.maximum(jnp.minimum(2 * t, t + 3), 2), jnp.minimum(2 * t + 2, t + 4), pass_on)
-        for j in range(2):
-            half_step(t, 1, j)
+            scores(task, first_block(first), 1, j)
+
+        @pl.when((turn == 0) & (z > 0))
+        def _():
+            start_gathers()
+
+        def half_step(t, h, j):
+            if h == 0:
+                weigh(task, first_block(t), 0, j)
+                gather_sums(task, second_block(jnp.maximum(t - 1, first)), 1, j)
+                scores(task, second_block(t), 0, j)
+            else:
+                weigh(task, second_block(t), 1, j)
+                gather_sums(task, first_block(t), 0, j)
+                scores(task, first_block(jnp.minimum(t + 1, end - 1)), 1, j)
+
+        def finish_unit(t):
+            done = t - first + begin
+
+            @pl.when((lax.rem(done, 2) == 1) & (done < gathered))
+            def _():
+                complete(region(done - 1))
+                complete(region(done))
+
+        def run_ahead(t):
+            n = t - first + begin
+            lead(n + 8 - 2 * jnp.maximum(1 - n, 0), n + 9, take_shard)
+            lead(jnp.minimum(2 * n + 4, n + 6), jnp.minimum(2 * n + 6, n + 7), take_line)
+            lead(
+                jnp.maximum(jnp.minimum(2 * n, n + 3), 2), jnp.minimum(2 * n + 2, n + 4), pass_on
+            )
+
+        def step(t, inner):
+            finish_unit(t)
+            for j in range(2):
+                half_step(t, 0, j)
+            run_ahead(t)
+            for j in range(2):
+                half_step(t, 1, j)
+            return inner
+
+        lax.fori_loop(first, end - 2, step, 0)
+
+        for j in (1, 0):
+
+            def last_step(t, inner):
+                if j == 1:
+                    finish_unit(t)
+                half_step(t, 0, j)
+                if j == 1:
+                    run_ahead(t)
+                half_step(t, 1, j)
+                return inner
+
+            lax.fori_loop(end - 2, end, last_step, 0)
+            gather_sums(task, second_block(end - 1), 1, j)
+            if j == 1:
+                ml[task, 0] = m_buf[1, :, ROWS:]
+                ml[task, 1] = l_buf[task, :, ROWS:]
+                for share in share_sums(task):
+                    share.start()
+
+                @pl.when((task == 0) & helper & (z > 0))
+                def _():
+                    pass_far_rows()
+        m_own[task] = m_buf[1, :, :ROWS]
+
+        @pl.when(task == 1)
+        def _():
+            peak, total, part_a, part_b = both_cores(1)
+            far_lse_out[...] = jnp.broadcast_to(peak + jnp.log2(total), (8, ROWS))
+            far_out[:HD] = (o1[1, 0, :HD, :] * part_a + o1_sib[1, :HD, :] * part_b).astype(HALF)
+            for copy in far_sums[:2]:
+                copy.start()
+            for share in share_sums(1)[2:]:
+                share.wait_recv()
+            far_out[HD : 2 * HD] = (o1[1, 0, HD:, :] * part_a + o1_sib[1, HD:, :] * part_b).astype(HALF)
+            far_out[2 * HD :] = (o2[1, 0] * part_a + o2_sib[1] * part_b).astype(HALF)
+            far_sums[2].start()
+
         return carry
 
-    lax.fori_loop(0, regions - 2, step, 0)
-
-    for j in (1, 0):
-
-        def last_step(t, carry):
-            if j == 1:
-                finish_unit(t)
-            half_step(t, 0, j)
-            half_step(t, 1, j)
-            return carry
-
-        lax.fori_loop(regions - 2, regions, last_step, 0)
-        gather_sums(second_block(regions - 1), 1, j)
-        if j == 1:
-            ml[0] = m_buf[1, :, ROWS:]
-            ml[1] = l_buf[:, ROWS:]
-            shares = [
-                remote(ml, ml_sib, core_send.at[1], core_recv.at[1], sibling),
-                remote(o1.at[1], o1_sib, core_send.at[2], core_recv.at[2], sibling),
-                remote(o2.at[1], o2_sib, core_send.at[3], core_recv.at[3], sibling),
-            ]
-            for share in shares:
-                share.start()
-
-    for share in shares:
-        share.wait_recv()
-    peak_a = m_buf[1, :1, :ROWS]
-    peak_b = ml_sib[0, :1, :]
-    peak = jnp.maximum(peak_a, peak_b)
-    part_a = jnp.exp2(peak_a - peak)
-    part_b = jnp.exp2(peak_b - peak)
-    total = part_a * jnp.sum(l_buf[:, :ROWS], axis=0, keepdims=True) + part_b * jnp.sum(
-        ml_sib[1], axis=0, keepdims=True
-    )
-    part_a = part_a / total
-    part_b = part_b / total
-    attended = (o1[0, :HD, :] * part_a + o1_sib[:HD, :] * part_b).astype(HALF)
-    delta = jnp.sum(gt[:, :ROWS].astype(FULL) * attended.astype(FULL), axis=0, keepdims=True)
+    lax.fori_loop(0, 2 - jnp.minimum(z // MOVED, 1), run, 0)
+
+    peak, total, part_a, part_b = both_cores(0)
+    lse = peak + jnp.log2(total)
+
+    @pl.when(helped)
+    def _():
+        for copy in far_sums[:2]:
+            copy.wait_recv()
+
+    @pl.when(jnp.logical_not(helped))
+    def _():
+        far[...] = jnp.zeros_like(far)
+        far_lse[...] = jnp.full_like(far_lse, -1e30)
+
+    peak = jnp.maximum(lse, far_lse[:1, :])
+    part_near = jnp.exp2(lse - peak)
+    part_far = jnp.exp2(far_lse[:1, :] - peak)
+    total = part_near + part_far
+    part_a = part_a * part_near / total
+    part_b = part_b * part_near / total
+    part_far = part_far / total
+    attended = (
+        o1[0, 0, :HD, :] * part_a + o1_sib[0, :HD, :] * part_b + far[:HD].astype(FULL) * part_far
+    ).astype(HALF)
+    delta = jnp.sum(gt[0, :, :ROWS].astype(FULL) * attended.astype(FULL), axis=0, keepdims=True)
     stats[0] = jnp.broadcast_to(peak + jnp.log2(total), (8, ROWS))
     stats[1] = jnp.broadcast_to(delta, (8, ROWS))
-    share_stats = remote(stats, stats_sib, core_send.at[4], core_recv.at[4], sibling)
+    share_stats = remote(stats, stats_sib, core_send.at[1], core_recv.at[1], sibling)
     share_stats.start()
 
-    mean_key = o1[0, HD:, :] * part_a + o1_sib[HD:, :] * part_b
-    qgrad = (o2[0] * part_a + o2_sib[...] * part_b - delta * mean_key) * scale
-    attended = attended.astype(FULL)
-    for h in range(HEADS):
-        cols = slice(h * HD, (h + 1) * HD)
-        gated[:, cols] = gain[:, cols] * attended[:, h * TOK : (h + 1) * TOK].T
-        query_grad[:, cols] = qgrad[:, h * TOK : (h + 1) * TOK].T
     def backward(p, line, cols, lse, drop):
         block = kv[p, pl.ds(pl.multiple_of(line * LINE, LINE), LINE), :]
-        prob = jnp.exp2(dot(block[:, HD:], qt[:, cols]) * to_log2 - lse)
-        dprob = dot(block[:, :HD], gt[:, cols])
+        prob = jnp.exp2(dot(block[:, HD:], qt[0, :, cols]) * to_log2 - lse)
+        dprob = dot(block[:, :HD], gt[0, :, cols])
         dscore = (prob * (dprob - drop) * scale).astype(HALF)
         vgrad = dot(prob.astype(HALF), g_rows[cols, :])
         kgrad = dot(dscore, q_rows[cols, :])
@@ -395,6 +549,11 @@
         own_part[p, :, :HD] = vgrad
         own_part[p, :, HD:] = kgrad
 
+    attended = attended.astype(FULL)
+    for h in range(HEADS):
+        cols = slice(h * HD, (h + 1) * HD)
+        gated[:, cols] = gain[:, cols] * attended[:, h * TOK : (h + 1) * TOK].T
+
     def piece_copy(p, d):
         _, v = place(p)
         at = pl.multiple_of(lax.rem(v + d, SIDE) * CUT, CUT)
@@ -412,6 +571,29 @@
         rs2_out[p] = own_part[p].astype(HALF)
         for d in range(1, SIDE):
             piece_copy(p, d).start()
+
+    for share in share_sums(0)[2:]:
+        share.wait_recv()
+
+    @pl.when(helped)
+    def _():
+        far_sums[2].wait_recv()
+
+    mean_key = (
+        o1[0, 0, HD:, :] * part_a
+        + o1_sib[0, HD:, :] * part_b
+        + far[HD : 2 * HD].astype(FULL) * part_far
+    )
+    qgrad = (
+        o2[0, 0] * part_a
+        + o2_sib[0] * part_b
+        + far[2 * HD :].astype(FULL) * part_far
+        - delta * mean_key
+    ) * scale
+    for h in range(HEADS):
+        cols = slice(h * HD, (h + 1) * HD)
+        query_grad[:, cols] = qgrad[:, h * TOK : (h + 1) * TOK].T
+
     for p in range(2):
         _, v = place(p)
         for d in range(1, SIDE):
@@ -421,30 +603,34 @@
         value_grad[pl.ds(p * CUT, CUT), :] = mine[:, :HD]
         key_grad[pl.ds(p * CUT, CUT), :] = mine[:, HD:]
 
-    for copy in [share_rows, share_stats] + shares:
+    for copy in [share_rows, share_stats] + share_sums(0):
         copy.wait_send()
+
+    @pl.when(helped)
+    def _():
+        far_rows.wait_send()
+
+    @pl.when(helper)
+    def _():
+        for copy in [pass_rows] + share_sums(1) + far_sums:
+            copy.wait_send()
+
     for p in range(2):
         for d in range(1, SIDE):
             part_copy(p, d).wait_send()
             piece_copy(p, d).wait_send()
 
-    def drain(r, carry):
+    def drain(order, carry):
+        r = region(order)
         line = line_at(r, 0)
         for sem in (up_send, down_send, s3_send):
             arrived(line, sem.at[r])
         arrived(kv.at[r, pl.ds(0, (SIDE - 1) * CUT)], s1_send.at[r])
         return carry
 
-    lax.fori_loop(0, regions, drain, 0)
-
-    def drain_shards(d, carry):
-        @pl.when(z + d < PLANES)
-        def _():
-            for p in range(2):
-                shard_copy(2 * d + p).wait_send()
-        return carry
-
-    lax.fori_loop(1, PLANES, drain_shards, 0)
+    lax.fori_loop(0, gathered, drain, 0)
+    each_shard(1, PLANES - MOVED, wait_send)
+    left_shard(wait_send)
 
 
 def body(query_in, key_in, value_in, clean_keys, clean_values, timestep, mod_table, out_grad):
@@ -470,8 +656,10 @@
             pltpu.VMEM((TOK, HEADS * HD), HALF),
             pltpu.VMEM((2, TOK, HEADS * HD), HALF),
             pltpu.VMEM((2, TOK, HEADS * HD), HALF),
-            pltpu.VMEM((HD, BOTH), HALF),
-            pltpu.VMEM((HD, BOTH), HALF),
+            pltpu.VMEM((2, TOK, HEADS * HD), HALF),
+            pltpu.VMEM((2, TOK, HEADS * HD), HALF),
+            pltpu.VMEM((2, HD, BOTH), HALF),
+            pltpu.VMEM((2, HD, BOTH), HALF),
             pltpu.VMEM((BOTH, HD), HALF),
             pltpu.VMEM((BOTH, HD), HALF),
             pltpu.VMEM((2, BK, BOTH), FULL),
@@ -479,13 +667,18 @@
             pltpu.VMEM((2, BK, BOTH), HALF),
             pltpu.VMEM((2, 8, BOTH), FULL),
             pltpu.VMEM((2, 8, BOTH), FULL),
-            pltpu.VMEM((8, BOTH), FULL),
+            pltpu.VMEM((2, 8, BOTH), FULL),
+            pltpu.VMEM((2, 8, ROWS), FULL),
+            pltpu.VMEM((2, 2, 2 * HD, ROWS), FULL),
+            pltpu.VMEM((2, 2, HD, ROWS), FULL),
+            pltpu.VMEM((2, 2, 8, ROWS), FULL),
+            pltpu.VMEM((2, 2, 8, ROWS), FULL),
             pltpu.VMEM((2, 2 * HD, ROWS), FULL),
             pltpu.VMEM((2, HD, ROWS), FULL),
-            pltpu.VMEM((2, 8, ROWS), FULL),
-            pltpu.VMEM((2, 8, ROWS), FULL),
-            pltpu.VMEM((2 * HD, ROWS), FULL),
-            pltpu.VMEM((HD, ROWS), FULL),
+            pltpu.VMEM((3 * HD, ROWS), HALF),
+            pltpu.VMEM((8, ROWS), FULL),
+            pltpu.VMEM((3 * HD, ROWS), HALF),
+            pltpu.VMEM((8, ROWS), FULL),
             pltpu.VMEM((2, 8, ROWS), FULL),
             pltpu.VMEM((2, 8, ROWS), FULL),
             pltpu.VMEM((2, SIDE - 1, LINE, 2 * HD), HALF),
@@ -494,8 +687,9 @@
             pltpu.VMEM((2, LINE, 2 * HD), HALF),
             pltpu.VMEM((2, SIDE - 1, CUT, 2 * HD), HALF),
             dma((11,)),
-            dma((5,)), dma((5,)),
-            dma((slots,)), dma((slots,)),
+            dma((11,)), dma((11,)),
+            dma((4,)), dma((4,)),
+            dma((2 * (PLANES - MOVED),)), dma((slots,)),
             dma((slots,)), dma((slots,)),
             dma((slots,)), dma((slots,)),
             dma((slots,)), dma((slots,)),

time: 92.6 us -> 80.3 us (0.87)
  Pallas kernels: 84.7 us -> 72.5 us
    pallas_call x1, Pallas kernels: 84.7 us -> 72.5 us  [body(): pl.pallas_call(kernel, name='attend', out_shape=[jax.ShapeDtypeStruct((TO...]
where the time goes in v3:
time: 80.3 us; the launch traced here: 80.1 us
  Pallas kernels  72.5 us (90%)
  local copies, waits for them, and re-layouts  6.29 us (8%)
  between operations  1.29 us (2%)
    pallas_call x1, Pallas kernels, body(): pl.pallas_call(kernel, name='attend', out_shape=[jax.ShapeDtypeStruct((TO...  72.5 us
    unnamed x4, local copies, waits for them, and re-layouts  6.29 us

profile of v3, /device:TPU:224, one launch (start us, length us, event | category | flops | bytes accessed | tf_op | source)
XLA Modules:
  0.0 80.1 jit_solution(15113094800255763777)
XLA Ops:
  1.3 72.5 %attend.1 = (f32[128,512]{1,0:T(8,128)}, f32[128,512]{1,0:T(8,128)}, f32[128,128]{1,0:T(8,128)}, f32[128,128]{1,0:T(8,128)}) custom-call(s32[1]{0:T(128)S(6)} %copy.16.timestep, bf16[128,512]{1,0:T(8,128)(2,1)} %query.1, bf16[128,128]{1,0:T(8,128)(2,1)} %key_in.1, bf16[128,128]{1,0:T(8,128)(2,1)} %value_in.1, bf16[128,128]{1,0:T(8,128)(2,1)} %clean_keys.1, ...), custom_call_target="tpu_custom_call" | custom-call | tf_op jit(solution)/shard_map/attend/pallas_call | solution.py:640
  73.8 1.7 %copy.17 = f32[128,512]{1,0:T(8,128)} copy(f32[128,512]{1,0:T(8,128)} %get-tuple-element.8) | data formatting | bytes 524288
  75.4 1.7 %copy.18 = f32[128,512]{1,0:T(8,128)} copy(f32[128,512]{1,0:T(8,128)} %get-tuple-element.9) | data formatting | bytes 524288
  77.1 1.5 %copy.19 = f32[128,128]{1,0:T(8,128)} copy(f32[128,128]{1,0:T(8,128)} %get-tuple-element.10) | data formatting | bytes 131072
  78.6 1.5 %copy.20 = f32[128,128]{1,0:T(8,128)} copy(f32[128,128]{1,0:T(8,128)} %get-tuple-element.11) | data formatting | bytes 131072

commit v4 on v3

--- a/solution.py
+++ b/solution.py
@@ -94,6 +94,15 @@
     def place(p):
         return p * x + (1 - p) * y, p * y + (1 - p) * x
 
+    barrier = pltpu.get_barrier_semaphore()
+    for d in range(1, SIDE):
+        pl.semaphore_signal(barrier, inc=1, device_id=chip(d, 0), device_id_type=MESH)
+        pl.semaphore_signal(barrier, inc=1, device_id=chip(0, d), device_id_type=MESH)
+    for d in range(1, PLANES):
+        pl.semaphore_signal(
+            barrier, inc=1, device_id=plane(lax.rem(z + d, PLANES)), device_id_type=MESH
+        )
+    pl.semaphore_signal(barrier, inc=1, device_id=sibling, device_id_type=MESH)
     loads = [
         pltpu.make_async_copy(query, qg.at[0], in_sem.at[0]),
         pltpu.make_async_copy(out_grad, grad_in, in_sem.at[1]),
@@ -122,15 +131,6 @@
     for load in shards + loads:
         load.start()
 
-    barrier = pltpu.get_barrier_semaphore()
-    for d in range(1, SIDE):
-        pl.semaphore_signal(barrier, inc=1, device_id=chip(d, 0), device_id_type=MESH)
-        pl.semaphore_signal(barrier, inc=1, device_id=chip(0, d), device_id_type=MESH)
-    for d in range(1, PLANES):
-        pl.semaphore_signal(
-            barrier, inc=1, device_id=plane(lax.rem(z + d, PLANES)), device_id_type=MESH
-        )
-    pl.semaphore_signal(barrier, inc=1, device_id=sibling, device_id_type=MESH)
     for load in shards:
         load.wait()
     pl.semaphore_wait(barrier, 2 * (SIDE - 1) + PLANES)
@@ -261,9 +261,10 @@
 
     each_shard(2, 3, start)
     lay_rows(qg, 0, 0)
+    each_shard(3, 4, start)
     for p in range(2):
         take_line(region(p))
-    each_shard(3, 4, start)
+    each_shard(4, PLANES - MOVED, start)
     share_rows.wait_recv()
     lay_rows(qg_sib, 0, ROWS)
 
@@ -367,7 +368,6 @@
         def start_gathers():
             for p in range(2):
                 pass_on(region(p))
-            each_shard(4, PLANES - MOVED, start)
 
             @pl.when(helped & (z < PLANES - 1))
             def _():
@@ -417,13 +417,18 @@
 
         def run_ahead(t):
             n = t - first + begin
-            lead(n + 8 - 2 * jnp.maximum(1 - n, 0), n + 9, take_shard)
-            lead(jnp.minimum(2 * n + 4, n + 6), jnp.minimum(2 * n + 6, n + 7), take_line)
+            lead(6 + 2 * jnp.minimum(n, 1), 8, take_shard)
             lead(
                 jnp.maximum(jnp.minimum(2 * n, n + 3), 2), jnp.minimum(2 * n + 2, n + 4), pass_on
             )
+            lead(jnp.minimum(2 * n + 4, n + 5), n + 6, take_line)
+
+        def take_next(t):
+            n = t - first + begin
+            lead(n + 7 + jnp.maximum(1 - n, 0), n + 8, take_shard)
 
         def step(t, inner):
+            take_next(t)
             finish_unit(t)
             for j in range(2):
                 half_step(t, 0, j)
@@ -438,6 +443,7 @@
 
             def last_step(t, inner):
                 if j == 1:
+                    take_next(t)
                     finish_unit(t)
                 half_step(t, 0, j)
                 if j == 1:
@@ -633,11 +639,17 @@
     left_shard(wait_send)
 
 
+def hand_over(*refs):
+    count = len(refs) // 2
+    for source, target in zip(refs[:count], refs[count:]):
+        target[...] = source[...]
+
+
 def body(query_in, key_in, value_in, clean_keys, clean_values, timestep, mod_table, out_grad):
     vmem = pl.BlockSpec(memory_space=pltpu.VMEM)
     dma = pltpu.SemaphoreType.DMA
     slots = 2 * PLANES
-    return pl.pallas_call(
+    found = pl.pallas_call(
         kernel,
         name="attend",
         out_shape=[
@@ -701,6 +713,13 @@
             collective_id=0, has_side_effects=True, vmem_limit_bytes=60 * 2**20
         ),
     )(timestep, query_in, key_in, value_in, clean_keys, clean_values, mod_table, out_grad)
+    return pl.pallas_call(
+        hand_over,
+        name="hand_over",
+        out_shape=[jax.ShapeDtypeStruct(one.shape, one.dtype) for one in found],
+        in_specs=[vmem] * 4,
+        out_specs=[vmem] * 4,
+    )(*found)
 
 
 def solution(mesh):

time: 80.3 us -> 73.4 us (0.914)
  the two profiles are of different devices: /device:TPU:224 before, /device:TPU:128 now
where the time goes in v4:
time: 73.4 us; the launch traced here: 73.3 us
  Pallas kernels  72 us (98%)
  between operations  1.29 us (2%)
    pallas_call x1, Pallas kernels, body(): pl.pallas_call(kernel, name='attend', out_shape=[jax.ShapeDtypeStruct((TO...  70.1 us
    pallas_call x1, Pallas kernels, body(): pl.pallas_call(hand_over, name='hand_over', out_shape=[jax.ShapeDtypeStru...  1.88 us

profile of v4, /device:TPU:128, one launch (start us, length us, event | category | flops | bytes accessed | tf_op | source)
XLA Modules:
  0.0 73.3 jit_solution(9515852090293630644)
XLA Ops:
  1.3 70.1 %attend.1 = (f32[128,512]{1,0:T(8,128)}, f32[128,512]{1,0:T(8,128)}, f32[128,128]{1,0:T(8,128)}, f32[128,128]{1,0:T(8,128)}) custom-call(s32[1]{0:T(128)S(6)} %copy.12.timestep, bf16[128,512]{1,0:T(8,128)(2,1)} %query.1, bf16[128,128]{1,0:T(8,128)(2,1)} %key_in.1, bf16[128,128]{1,0:T(8,128)(2,1)} %value_in.1, bf16[128,128]{1,0:T(8,128)(2,1)} %clean_keys.1, ...), custom_call_target="tpu_custom_call" | custom-call | tf_op jit(solution)/shard_map/attend/pallas_call | solution.py:652
  71.4 1.9 %hand_over.1 = (f32[128,512]{1,0:T(8,128)}, f32[128,512]{1,0:T(8,128)}, f32[128,128]{1,0:T(8,128)}, f32[128,128]{1,0:T(8,128)}) custom-call(f32[128,512]{1,0:T(8,128)} %get-tuple-element.8.refs_0_, f32[128,512]{1,0:T(8,128)} %get-tuple-element.9.refs_1_, f32[128,128]{1,0:T(8,128)} %get-tuple-element.10.refs_2_, f32[128,128]{1,0:T(8,128)} %get-tuple-element.11.refs_3_), custom_call_target="tpu_custom_call" | custom-call | tf_op jit(solution)/shard_map/hand_over/pallas_call | solution.py:716

commit v5 on v4

--- a/solution.py
+++ b/solution.py
@@ -397,7 +397,7 @@
         def _():
             start_gathers()
 
-        def half_step(t, h, j):
+        def half_step(t, h, j, final=False):
             if h == 0:
                 weigh(task, first_block(t), 0, j)
                 gather_sums(task, second_block(jnp.maximum(t - 1, first)), 1, j)
@@ -405,7 +405,8 @@
             else:
                 weigh(task, second_block(t), 1, j)
                 gather_sums(task, first_block(t), 0, j)
-                scores(task, first_block(jnp.minimum(t + 1, end - 1)), 1, j)
+                if not final:
+                    scores(task, first_block(jnp.minimum(t + 1, end - 1)), 1, j)
 
         def finish_unit(t):
             done = t - first + begin
@@ -440,18 +441,15 @@
         lax.fori_loop(first, end - 2, step, 0)
 
         for j in (1, 0):
-
-            def last_step(t, inner):
+            for back in (2, 1):
+                t = end - back
                 if j == 1:
                     take_next(t)
                     finish_unit(t)
                 half_step(t, 0, j)
                 if j == 1:
                     run_ahead(t)
-                half_step(t, 1, j)
-                return inner
-
-            lax.fori_loop(end - 2, end, last_step, 0)
+                half_step(t, 1, j, final=back == 1)
             gather_sums(task, second_block(end - 1), 1, j)
             if j == 1:
                 ml[task, 0] = m_buf[1, :, ROWS:]

time: 73.4 us -> 72.7 us (level)
  Pallas kernels: 72 us -> 71.2 us
    pallas_call x1, Pallas kernels: 70.1 us -> 69.3 us  [body(): pl.pallas_call(kernel, name='attend', out_shape=[jax.ShapeDtypeStruct((TO...]
where the time goes in v5:
time: 72.7 us; the launch traced here: 72.5 us
  Pallas kernels  71.2 us (98%)
  between operations  1.29 us (2%)
    pallas_call x1, Pallas kernels, body(): pl.pallas_call(kernel, name='attend', out_shape=[jax.ShapeDtypeStruct((TO...  69.3 us
    pallas_call x1, Pallas kernels, body(): pl.pallas_call(hand_over, name='hand_over', out_shape=[jax.ShapeDtypeStru...  1.88 us

profile of v5, /device:TPU:128, one launch (start us, length us, event | category | flops | bytes accessed | tf_op | source)
XLA Modules:
  0.0 72.5 jit_solution(9957945844509773571)
XLA Ops:
  1.3 69.3 %attend.1 = (f32[128,512]{1,0:T(8,128)}, f32[128,512]{1,0:T(8,128)}, f32[128,128]{1,0:T(8,128)}, f32[128,128]{1,0:T(8,128)}) custom-call(s32[1]{0:T(128)S(6)} %copy.12.timestep, bf16[128,512]{1,0:T(8,128)(2,1)} %query.1, bf16[128,128]{1,0:T(8,128)(2,1)} %key_in.1, bf16[128,128]{1,0:T(8,128)(2,1)} %value_in.1, bf16[128,128]{1,0:T(8,128)(2,1)} %clean_keys.1, ...), custom_call_target="tpu_custom_call" | custom-call | tf_op jit(solution)/shard_map/attend/pallas_call | solution.py:650
  70.6 1.9 %hand_over.1 = (f32[128,512]{1,0:T(8,128)}, f32[128,512]{1,0:T(8,128)}, f32[128,128]{1,0:T(8,128)}, f32[128,128]{1,0:T(8,128)}) custom-call(f32[128,512]{1,0:T(8,128)} %get-tuple-element.8.refs_0_, f32[128,512]{1,0:T(8,128)} %get-tuple-element.9.refs_1_, f32[128,128]{1,0:T(8,128)} %get-tuple-element.10.refs_2_, f32[128,128]{1,0:T(8,128)} %get-tuple-element.11.refs_3_), custom_call_target="tpu_custom_call" | custom-call | tf_op jit(solution)/shard_map/hand_over/pallas_call | solution.py:714
